TPU v7x, 32 devices: a whole 2x2x4 slice. The times are simulated.
32 devices in a mesh: groups: 2 (over x), seq: 16 (over z, y, core).
Axes of the slice: x: 2, y: 2, z: 4, core: 2. Of those that a mesh axis runs over, the one named last changes fastest.
Arguments:
- tokens: int32 [16384], P(('groups', 'seq')), parts along dimension 0, may hold values from 0 to 3
- dilations: int32 [2], replicated, may hold values from 1 to 64, as said below
- embedding: bfloat16 [4, 512], replicated, may hold values from -6 to 6
- norm_gain: float32 [2, 512], replicated, may hold values from 0.1 to 1.9
- conv_taps: float32 [2, 3, 512], replicated, may hold values from -3 to 3
- w_up: bfloat16 [2, 512, 512], replicated, may hold values from -0.25 to 0.25
- w_gate: bfloat16 [2, 512, 512], replicated, may hold values from -0.25 to 0.25
- w_out: bfloat16 [2, 512, 512], replicated, may hold values from -0.25 to 0.25
- cotangent: bfloat16 [16384, 512], P(('groups', 'seq')), parts along dimension 0, may hold values from -6 to 6
Outputs:
- grad_up: float32 [4, 512, 512], P('groups', None, 'seq'), parts along dimension 0
- grad_gate: float32 [4, 512, 512], P('groups', None, 'seq'), parts along dimension 0
- grad_out: float32 [4, 512, 512], P('groups', None, 'seq'), parts along dimension 0
- grad_taps: float32 [4, 3, 512], P('groups'), parts along dimension 0
- grad_gain: float32 [4, 512], P('groups'), parts along dimension 0
- grad_embed: float32 [8, 512], P('groups'), parts along dimension 0
There are 2 independent parts, one for each index of `groups`. A program takes and returns all parts, laid end to end along the dimension named above; an argument that names none is the same for every part. Nothing has to cross between parts.
Inputs may be any that keep to these rules, and one draw needn't show every extreme that they name: `dilations`: at least one block has dilation exactly 64.
All inputs are finite; a program needn't handle non-finite values.
Results may differ from a plain program's by a relative error of at most 0.014.
Values may be sent and summed in bfloat16 or wider, within the bound.
A program may use at most 64 MiB of HBM per device.

v0:
```python
import jax
import jax.numpy as jnp
from jax import lax
from jax.sharding import PartitionSpec as P

DMAX = 64


EPSILON = 1e-06


def with_halo(shard, sides, width):
    for axis, dim in sides:
        devices, length = (lax.axis_size(axis), shard.shape[dim])
        up = [(i, (i + 1) % devices) for i in range(devices - 1)]
        down = [(j, i) for i, j in up]
        last = lax.slice_in_dim(shard, length - width, length, axis=dim)
        leading = lax.slice_in_dim(shard, 0, width, axis=dim)
        before = lax.ppermute(last, axis, up)
        after = lax.ppermute(leading, axis, down)
        shard = jnp.concatenate([before, shard, after], axis=dim)
    return shard


def shifted(padded, tapset, dilation, row_count, direction):
    summed = jnp.zeros((padded.shape[0], row_count, padded.shape[2]), jnp.float32)
    for offset in range(3):
        window = lax.dynamic_slice_in_dim(
            padded, DMAX + direction * (offset - 1) * dilation, row_count, 1
        ).astype(jnp.float32)
        summed = summed + tapset[:, offset][:, None, :] * window
    return summed


def contract_rows(former, latter, accuracy=None):
    return lax.dot_general(
        former,
        latter,
        (((0,), (0,)), ((), ())),
        preferred_element_type=jnp.float32,
        precision=accuracy,
    )


def mirror(block):
    parts_count = lax.axis_size("seq")
    row_count, channels = block.shape
    pieces = jnp.flip(block, 0).reshape(parts_count, row_count // parts_count, channels)
    pieces = lax.all_to_all(pieces, "seq", split_axis=0, concat_axis=0, tiled=True)
    pieces = jnp.flip(pieces, 0)
    pieces = lax.all_to_all(pieces, "seq", split_axis=0, concat_axis=0, tiled=True)
    return pieces.reshape(row_count, channels)


def per_device(tokens, dilations, embedding, norm_gain, conv_taps, w_up, w_gate, w_out, cotangent):
    row_count = tokens.shape[0]
    layer_count = dilations.shape[0]
    one_hot = tokens[:, None] == jnp.arange(4, dtype=jnp.int32)[None, :]
    initial = jnp.dot(
        one_hot.astype(jnp.bfloat16), embedding, preferred_element_type=jnp.float32
    ).astype(jnp.bfloat16)
    state = initial[None]
    gradient = cotangent[None].astype(jnp.float32)
    saved = []
    for layer_at in range(layer_count):
        dilation = dilations[layer_at]
        tapset = conv_taps[layer_at][None]
        wide = state.astype(jnp.float32)
        inverse = lax.rsqrt(jnp.mean(wide * wide, axis=-1, keepdims=True) + EPSILON)
        unit = wide * inverse
        normed = (unit * norm_gain[layer_at]).astype(jnp.bfloat16)
        padded = with_halo(normed, (("seq", 1),), DMAX)
        mixed = shifted(padded, tapset, dilation, row_count, 1).astype(jnp.bfloat16)
        partner = mirror(normed[0])[None]
        upward = jnp.einsum(
            "krc,cf->krf", mixed, w_up[layer_at], preferred_element_type=jnp.float32
        )
        gate_sig = jax.nn.sigmoid(
            jnp.einsum("krc,cf->krf", partner, w_gate[layer_at], preferred_element_type=jnp.float32)
        )
        hidden = (upward * gate_sig).astype(jnp.bfloat16)
        saved.append(
            (unit, inverse, padded, mixed, partner, upward, gate_sig, hidden, tapset, dilation)
        )
        if layer_at + 1 < layer_count:
            state = (
                wide
                + jnp.einsum(
                    "krf,fc->krc", hidden, w_out[layer_at], preferred_element_type=jnp.float32
                )
            ).astype(jnp.bfloat16)
    up_list, gate_list, out_list, tap_list, gain_list = ([], [], [], [], [])
    for layer_at in reversed(range(layer_count)):
        unit, inverse, padded, mixed, partner, upward, gate_sig, hidden, tapset, dilation = saved[
            layer_at
        ]
        grad_low = gradient.astype(jnp.bfloat16)
        grad_hidden = jnp.einsum(
            "krc,fc->krf", grad_low, w_out[layer_at], preferred_element_type=jnp.float32
        )
        grad_upward = (grad_hidden * gate_sig).astype(jnp.bfloat16)
        grad_logit = (grad_hidden * upward * gate_sig * (1.0 - gate_sig)).astype(jnp.bfloat16)
        term_out = contract_rows(hidden[0], grad_low[0])
        term_up = contract_rows(mixed[0], grad_upward[0])
        term_gate = contract_rows(partner[0], grad_logit[0])
        up_list.append(term_up)
        gate_list.append(term_gate)
        out_list.append(term_out)
        grad_mixed = jnp.einsum(
            "krf,cf->krc", grad_upward, w_up[layer_at], preferred_element_type=jnp.float32
        ).astype(jnp.bfloat16)
        grad_partner = jnp.einsum(
            "krf,cf->krc", grad_logit, w_gate[layer_at], preferred_element_type=jnp.float32
        ).astype(jnp.bfloat16)
        returned = mirror(grad_partner[0])[None]
        grad_pad = with_halo(grad_mixed, (("seq", 1),), DMAX)
        grad_normed = shifted(grad_pad, tapset, dilation, row_count, -1) + returned.astype(
            jnp.float32
        )
        grad_own = grad_mixed[0].astype(jnp.float32)
        tap_rows = []
        for offset in range(3):
            window = lax.dynamic_slice_in_dim(
                padded[0], DMAX + (offset - 1) * dilation, row_count, 0
            ).astype(jnp.float32)
            tap_rows.append(jnp.sum(grad_own * window, axis=0))
        tap_list.append(jnp.stack(tap_rows))
        gain_list.append(jnp.sum(grad_normed[0] * unit[0], axis=0))
        grad_unit = grad_normed * norm_gain[layer_at]
        gradient = gradient + inverse * (
            grad_unit - unit * jnp.mean(grad_unit * unit, axis=-1, keepdims=True)
        )
    embed_term = contract_rows(one_hot.astype(jnp.float32), gradient[0], lax.Precision.HIGHEST)
    grad_up, grad_gate, grad_out = (
        lax.psum_scatter(jnp.stack(up_list[::-1]), "seq", scatter_dimension=2, tiled=True),
        lax.psum_scatter(jnp.stack(gate_list[::-1]), "seq", scatter_dimension=2, tiled=True),
        lax.psum_scatter(jnp.stack(out_list[::-1]), "seq", scatter_dimension=2, tiled=True),
    )
    grad_taps, grad_gain, grad_embed = lax.psum(
        (jnp.stack(tap_list[::-1]), jnp.stack(gain_list[::-1]), embed_term), "seq"
    )
    return (grad_up, grad_gate, grad_out, grad_taps, grad_gain, grad_embed)


def solution(mesh):
    in_specs = (P(("groups", "seq")), P(), P(), P(), P(), P(), P(), P(), P(("groups", "seq"), None))
    out_specs = (
        P("groups", None, "seq"),
        P("groups", None, "seq"),
        P("groups", None, "seq"),
        P("groups", None, None),
        P("groups", None),
        P("groups", None),
    )
    return jax.shard_map(
        per_device, mesh=mesh, in_specs=in_specs, out_specs=out_specs, check_vma=False
    )
```

profile of v0, /device:TPU:0, one launch (start us, length us, event | category | flops | bytes accessed | tf_op | source)
XLA Modules:
  0.0 363.0 jit_solution(13554539525253559118)
XLA Ops:
  8.0 1.1 fusion.41
  10.0 21.7 %all_to_all.40 = bf16[16,32,512]{2,1,0:T(8,128)(2,1)S(1)} all-to-all(bf16[16,32,512]{2,1,0:T(8,128)(2,1)S(1)} %bitcast.234), channel_id=1, replica_groups=mesh['groups'=2,'seq'=16] {'seq'}, dimensions={0} | all-to-all | bytes 1048576 | tf_op jit(solution)/shard_map/all_to_all | solution.py:49
  32.4 4.1 %all-to-all-start.1 = ((bf16[16,32,512]{2,1,0:T(8,128)(2,1)}), bf16[16,32,512]{2,1,0:T(8,128)(2,1)S(1)}, u32[]{:S(2)}, u32[]{:S(2)}) async-start(bf16[16,32,512]{2,1,0:T(8,128)(2,1)} %rev.18), calls=%async_computation.1 | async-start | bytes 1048576 | tf_op jit(solution)/shard_map/all_to_all | solution.py:51
  36.8 2.4 collective-permute-start
  39.2 1.3 collective-permute-start.1
  45.0 6.0 %all-to-all-done.1 = bf16[16,32,512]{2,1,0:T(8,128)(2,1)S(1)} async-done(((bf16[16,32,512]{2,1,0:T(8,128)(2,1)}), bf16[16,32,512]{2,1,0:T(8,128)(2,1)S(1)}, u32[]{:S(2)}, u32[]{:S(2)}) %all-to-all-start.1) | async-done | bytes 524320 | tf_op jit(solution)/shard_map/all_to_all | solution.py:51
  53.1 1.4 multiply_convert_fusion.5
  55.8 5.1 %reverse.13 = bf16[512,512]{1,0:T(8,128)(2,1)} reverse(bf16[512,512]{1,0:T(8,128)(2,1)S(1)} %fusion.19), dimensions={0} | reverse | bytes 1048576 | tf_op jit(solution)/shard_map/reverse.1
  61.0 6.0 %all-to-all-start.2 = ((bf16[16,32,512]{2,1,0:T(8,128)(2,1)}), bf16[16,32,512]{2,1,0:T(8,128)(2,1)S(1)}, u32[]{:S(2)}, u32[]{:S(2)}) async-start(bf16[16,32,512]{2,1,0:T(8,128)(2,1)} %bitcast.231), calls=%async_computation.2 | async-start | bytes 1048576 | tf_op jit(solution)/shard_map/all_to_all | solution.py:49
  67.2 14.3 %all-to-all-done.2 = bf16[16,32,512]{2,1,0:T(8,128)(2,1)S(1)} async-done(((bf16[16,32,512]{2,1,0:T(8,128)(2,1)}), bf16[16,32,512]{2,1,0:T(8,128)(2,1)S(1)}, u32[]{:S(2)}, u32[]{:S(2)}) %all-to-all-start.2) | async-done | bytes 524320 | tf_op jit(solution)/shard_map/all_to_all | solution.py:49
  82.3 4.2 %all-to-all-start.3 = ((bf16[16,32,512]{2,1,0:T(8,128)(2,1)}), bf16[16,32,512]{2,1,0:T(8,128)(2,1)}, u32[]{:S(2)}, u32[]{:S(2)}) async-start(bf16[16,32,512]{2,1,0:T(8,128)(2,1)} %rev.19), calls=%async_computation.3 | async-start | bytes 1048576 | tf_op jit(solution)/shard_map/all_to_all | solution.py:51
  86.5 2.2 collective-permute-start.4
  88.7 1.3 collective-permute-start.5
  90.0 2.5 fusion.69
  96.9 2.5 fusion.64
  99.4 1.6 all-to-all-done.3
  101.0 3.8 %multiply_convert_fusion.3 = (bf16[512,512]{1,0:T(8,128)(2,1)S(1)}, bf16[512,512]{1,0:T(8,128)(2,1)}, f32[512,512]{1,0:T(8,128)}) fusion(f32[512,512]{1,0:T(8,128)} %fusion.69, f32[512,512]{1,0:T(8,128)} %fusion.64, bf16[512,512]{1,0:T(8,128)(2,1)} %bitcast.21, bf16[2,512,512]{2,1,0:T(8,128)(2,1)} %param.15), kind=kOutput, calls=%fused_computation.98 | convolution fusion | flops 271056896 | bytes 5242880 | tf_op jit(solution)/shard_map/krc,cf->krf/dot_general | solution.py:79
  105.6 1.3 convolution_convert_fusion.2
  106.9 8.3 %reverse.14 = bf16[512,512]{1,0:T(8,128)(2,1)} reverse(bf16[512,512]{1,0:T(8,128)(2,1)} %convolution_convert_fusion.2), dimensions={0} | reverse | bytes 1048576 | tf_op jit(solution)/shard_map/reverse.2
  115.2 23.7 %all_to_all.41 = bf16[16,32,512]{2,1,0:T(8,128)(2,1)} all-to-all(bf16[16,32,512]{2,1,0:T(8,128)(2,1)} %bitcast.232), channel_id=1, replica_groups=mesh['groups'=2,'seq'=16] {'seq'}, dimensions={0} | all-to-all | bytes 1048576 | tf_op jit(solution)/shard_map/all_to_all | solution.py:49
  138.9 1.9 rev.20
  140.8 4.2 %all-to-all-start.5 = ((bf16[16,32,512]{2,1,0:T(8,128)(2,1)}), bf16[16,32,512]{2,1,0:T(8,128)(2,1)}, u32[]{:S(2)}, u32[]{:S(2)}) async-start(bf16[16,32,512]{2,1,0:T(8,128)(2,1)} %rev.20), calls=%async_computation.5 | async-start | bytes 1048576 | tf_op jit(solution)/shard_map/all_to_all | solution.py:51
  145.1 1.8 convolution_convert_fusion.3
  147.0 2.2 collective-permute-start.2
  149.1 1.5 collective-permute-start.3
  150.6 2.6 convolution_bitcast_fusion.4
  153.3 1.5 convolution_bitcast_fusion
  154.8 2.5 convolution_bitcast_fusion.2
  158.2 1.3 all-to-all-done.5
  159.5 2.7 fusion.46
  163.2 1.6 convolution_bitcast_fusion.1
  165.1 1.4 multiply_convert_fusion.1
  167.9 1.5 pad_maximum_fusion.1
  169.4 4.2 %copy.23 = f32[2,512,512]{1,0,2:T(2,128)} copy(f32[2,512,512]{2,1,0:T(8,128)} %pad_maximum_fusion.1) | data formatting | bytes 4194304 | tf_op jit(solution)/shard_map/stack | solution.py:136
  173.6 2.9 pad_maximum_fusion.2
  176.5 4.2 %copy.24 = f32[2,512,512]{1,0,2:T(2,128)} copy(f32[2,512,512]{2,1,0:T(8,128)} %pad_maximum_fusion.2) | data formatting | bytes 4194304 | tf_op jit(solution)/shard_map/stack | solution.py:137
  181.9 1.6 pad_maximum_fusion
  183.5 4.1 %copy.22 = f32[2,512,512]{1,0,2:T(2,128)} copy(f32[2,512,512]{2,1,0:T(8,128)} %pad_maximum_fusion) | data formatting | bytes 4194304 | tf_op jit(solution)/shard_map/stack | solution.py:135
  188.6 1.5 convolution_convert_fusion
  190.8 29.5 %all_to_all.42 = bf16[16,32,512]{2,1,0:T(8,128)(2,1)S(1)} all-to-all(bf16[16,32,512]{2,1,0:T(8,128)(2,1)S(1)} %bitcast.233), channel_id=1, replica_groups=mesh['groups'=2,'seq'=16] {'seq'}, dimensions={0} | all-to-all | bytes 1048576 | tf_op jit(solution)/shard_map/all_to_all | solution.py:49
  221.2 3.6 all-to-all-start.7
  226.0 2.2 fusion.49
  228.2 2.2 collective-permute-start.6
  230.4 1.3 collective-permute-start.7
  231.8 3.0 collective-permute-done.7
  234.8 13.0 %all-to-all-done.7 = bf16[16,32,512]{2,1,0:T(8,128)(2,1)S(1)} async-done(((bf16[16,32,512]{2,1,0:T(8,128)(2,1)}), bf16[16,32,512]{2,1,0:T(8,128)(2,1)S(1)}, u32[]{:S(2)}, u32[]{:S(2)}) %all-to-all-start.7) | async-done | bytes 524320 | tf_op jit(solution)/shard_map/all_to_all | solution.py:51
  249.8 58.4 %all-reduce.3 = (f32[2,3,512]{2,1,0:T(4,128)S(1)}, f32[2,512]{1,0:T(2,128)}, f32[4,512]{1,0:T(4,128)}) all-reduce(f32[2,3,512]{2,1,0:T(4,128)S(1)} %pad_maximum_fusion.7, f32[2,512]{1,0:T(2,128)S(1)} %pad_maximum_fusion.8, f32[4,512]{1,0:T(4,128)S(1)} %fusion.56), channel_id=1, replica_groups=mesh['groups'=2,'seq'=16] {'seq'}, use_global_device_ids=true, to_apply=%region_12.13 | all-reduce | flops 6144 | bytes 49152 | tf_op jit(solution)/shard_map/psum | solution.py:139
  308.9 43.4 %all-reduce.7.cloned.1.call-done = (f32[2,512,512]{1,0,2:T(2,128)}, f32[2,512,512]{1,0,2:T(2,128)}, f32[2,512,512]{1,0,2:T(2,128)}) async-done(((f32[2,512,512]{1,0,2:T(2,128)}, f32[2,512,512]{1,0,2:T(2,128)}, f32[2,512,512]{1,0,2:T(2,128)}), (f32[2,512,512]{1,0,2:T(2,128)}, f32[2,512,512]{1,0,2:T(2,128)}, f32[2,512,512]{1,0,2:T(2,128)})) %all-reduce.7.cloned.1.call-update) | async-done | bytes 6291472
  (122 shorter events, 27.5 us)
Async XLA Ops:
  7.2 0.8 copy-start
  9.3 23.2 %copy-start.16 = (bf16[512,512]{1,0:T(8,128)(2,1)}, bf16[512,512]{1,0:T(8,128)(2,1)S(1)}, u32[]{:S(2)}) copy-start(bf16[512,512]{1,0:T(8,128)(2,1)S(1)} %fusion.32) | copy-start | bytes 1572868
  9.9 30.6 %copy-start.28 = (f32[2,3,512]{2,0,1:T(2,128)S(1)}, f32[2,3,512]{2,0,1:T(2,128)}, u32[]{:S(2)}) copy-start(f32[2,3,512]{2,0,1:T(2,128)} %param.13) | copy-start | bytes 36868
  9.9 30.6 %copy-start.29 = (s32[2]{0:T(128)S(1)}, s32[2]{0:T(128)}, u32[]{:S(2)}) copy-start(s32[2]{0:T(128)} %param.10) | copy-start | bytes 28
  32.4 18.6 %all-to-all-start.1 = ((bf16[16,32,512]{2,1,0:T(8,128)(2,1)}), bf16[16,32,512]{2,1,0:T(8,128)(2,1)S(1)}, u32[]{:S(2)}, u32[]{:S(2)}) async-start(bf16[16,32,512]{2,1,0:T(8,128)(2,1)} %rev.18), calls=%async_computation.1 | async-start | bytes 1048576 | tf_op jit(solution)/shard_map/all_to_all | solution.py:51
  36.7 15.1 %copy-start.31 = (bf16[2,512,512]{2,1,0:T(8,128)(2,1)S(1)}, bf16[2,512,512]{2,1,0:T(8,128)(2,1)}, u32[]{:S(2)}) copy-start(bf16[2,512,512]{2,1,0:T(8,128)(2,1)} %param.15) | copy-start | bytes 3145732
  36.8 6.3 %collective-permute-start = (bf16[1,64,512]{2,1,0:T(8,128)(2,1)S(1)}, bf16[1,64,512]{2,1,0:T(8,128)(2,1)S(1)}, u32[]{:S(2)}, u32[]{:S(2)}) collective-permute-start(bf16[1,64,512]{2,1,0:T(8,128)(2,1)S(1)} %get-tuple-element.52), channel_id=1, source_target_pairs={{0,1},{1,2},{2,3},{3,4},{4,5},{5,6},{6,7},{7,8},{8,9},{9,10},{10,1... | collective-permute-start | bytes 196616 | tf_op jit(solution)/shard_map/ppermute | solution.py:19
  39.2 4.3 %collective-permute-start.1 = (bf16[1,64,512]{2,1,0:T(8,128)(2,1)S(1)}, bf16[1,64,512]{2,1,0:T(8,128)(2,1)S(1)}, u32[]{:S(2)}, u32[]{:S(2)}) collective-permute-start(bf16[1,64,512]{2,1,0:T(8,128)(2,1)S(1)} %get-tuple-element.53), channel_id=1, source_target_pairs={{1,0},{2,1},{3,2},{4,3},{5,4},{6,5},{7,6},{8,7},{9,8},{10,9},{11,1... | collective-permute-start | bytes 196616 | tf_op jit(solution)/shard_map/ppermute | solution.py:20
  43.6 0.9 copy-start.3
  51.0 0.8 copy-start.20
  51.9 1.2 copy-start.25
  53.1 2.5 copy-start.6
  53.1 2.0 copy-start.23
  54.5 6.5 %copy-start.14 = (bf16[512,512]{1,0:T(8,128)(2,1)}, bf16[512,512]{1,0:T(8,128)(2,1)S(1)}, u32[]{:S(2)}) copy-start(bf16[512,512]{1,0:T(8,128)(2,1)S(1)} %get-tuple-element.66) | copy-start | bytes 1572868
  61.0 29.1 %copy-start.1 = (bf16[512,512]{1,0:T(8,128)(2,1)S(1)}, bf16[512,512]{1,0:T(8,128)(2,1)}, u32[]{:S(2)}) copy-start(bf16[512,512]{1,0:T(8,128)(2,1)} %param.17) | copy-start | bytes 1572868
  61.0 20.5 %all-to-all-start.2 = ((bf16[16,32,512]{2,1,0:T(8,128)(2,1)}), bf16[16,32,512]{2,1,0:T(8,128)(2,1)S(1)}, u32[]{:S(2)}, u32[]{:S(2)}) async-start(bf16[16,32,512]{2,1,0:T(8,128)(2,1)} %bitcast.231), calls=%async_computation.2 | async-start | bytes 1048576 | tf_op jit(solution)/shard_map/all_to_all | solution.py:49
  67.1 25.4 %copy-start.13 = (bf16[1,512,512]{2,1,0:T(8,128)(2,1)}, bf16[1,512,512]{2,1,0:T(8,128)(2,1)S(1)}, u32[]{:S(2)}) copy-start(bf16[1,512,512]{2,1,0:T(8,128)(2,1)S(1)} %fusion.106) | copy-start | bytes 1572868
  82.3 18.7 %all-to-all-start.3 = ((bf16[16,32,512]{2,1,0:T(8,128)(2,1)}), bf16[16,32,512]{2,1,0:T(8,128)(2,1)}, u32[]{:S(2)}, u32[]{:S(2)}) async-start(bf16[16,32,512]{2,1,0:T(8,128)(2,1)} %rev.19), calls=%async_computation.3 | async-start | bytes 1048576 | tf_op jit(solution)/shard_map/all_to_all | solution.py:51
  86.5 7.9 %collective-permute-start.4 = (bf16[1,64,512]{2,1,0:T(8,128)(2,1)S(1)}, bf16[1,64,512]{2,1,0:T(8,128)(2,1)S(1)}, u32[]{:S(2)}, u32[]{:S(2)}) collective-permute-start(bf16[1,64,512]{2,1,0:T(8,128)(2,1)S(1)} %get-tuple-element.50), channel_id=1, source_target_pairs={{0,1},{1,2},{2,3},{3,4},{4,5},{5,6},{6,7},{7,8},{8,9},{9,10},{10,1... | collective-permute-start | bytes 196616 | tf_op jit(solution)/shard_map/ppermute | solution.py:19
  88.7 5.8 %collective-permute-start.5 = (bf16[1,64,512]{2,1,0:T(8,128)(2,1)S(1)}, bf16[1,64,512]{2,1,0:T(8,128)(2,1)S(1)}, u32[]{:S(2)}, u32[]{:S(2)}) collective-permute-start(bf16[1,64,512]{2,1,0:T(8,128)(2,1)S(1)} %get-tuple-element.51), channel_id=1, source_target_pairs={{1,0},{2,1},{3,2},{4,3},{5,4},{6,5},{7,6},{8,7},{9,8},{10,9},{11,1... | collective-permute-start | bytes 196616 | tf_op jit(solution)/shard_map/ppermute | solution.py:20
  96.1 0.8 copy-start.2
  101.0 4.6 %copy-start.32 = (bf16[2,512,512]{2,1,0:T(8,128)(2,1)S(1)}, bf16[2,512,512]{2,1,0:T(8,128)(2,1)}, u32[]{:S(2)}) copy-start(bf16[2,512,512]{2,1,0:T(8,128)(2,1)} %param.15) | copy-start | bytes 3145732
  104.8 0.8 copy-start.26
  140.8 18.7 %all-to-all-start.5 = ((bf16[16,32,512]{2,1,0:T(8,128)(2,1)}), bf16[16,32,512]{2,1,0:T(8,128)(2,1)}, u32[]{:S(2)}, u32[]{:S(2)}) async-start(bf16[16,32,512]{2,1,0:T(8,128)(2,1)} %rev.20), calls=%async_computation.5 | async-start | bytes 1048576 | tf_op jit(solution)/shard_map/all_to_all | solution.py:51
  145.0 207.2 %all-reduce.7.cloned.1.call-start = ((), (), s32[]{:S(2)}) async-start(), calls=%async_computation.8 | async-start | bytes 12582912
  145.1 8.2 %copy-start.5 = (f32[512,512]{1,0:T(8,128)S(1)}, f32[512,512]{1,0:T(8,128)}, u32[]{:S(2)}) copy-start(f32[512,512]{1,0:T(8,128)} %fusion.64) | copy-start | bytes 3145732
  145.1 8.2 %copy-start.22 = (f32[512,512]{1,0:T(8,128)S(1)}, f32[512,512]{1,0:T(8,128)}, u32[]{:S(2)}) copy-start(f32[512,512]{1,0:T(8,128)} %get-tuple-element.70) | copy-start | bytes 3145732
  146.9 10.4 %copy-start.12 = (bf16[512,512]{1,0:T(8,128)(2,1)}, bf16[512,512]{1,0:T(8,128)(2,1)S(1)}, u32[]{:S(2)}) copy-start(bf16[512,512]{1,0:T(8,128)(2,1)S(1)} %convolution_convert_fusion.3) | copy-start | bytes 1572868
  147.0 10.4 %collective-permute-start.2 = (bf16[1,64,512]{2,1,0:T(8,128)(2,1)S(1)}, bf16[1,64,512]{2,1,0:T(8,128)(2,1)S(1)}, u32[]{:S(2)}, u32[]{:S(2)}) collective-permute-start(bf16[1,64,512]{2,1,0:T(8,128)(2,1)S(1)} %get-tuple-element.48), channel_id=1, source_target_pairs={{0,1},{1,2},{2,3},{3,4},{4,5},{5,6},{6,7},{7,8},{8,9},{9,10},{10,1... | collective-permute-start | bytes 196616 | tf_op jit(solution)/shard_map/ppermute | solution.py:19
  149.1 8.2 %collective-permute-start.3 = (bf16[1,64,512]{2,1,0:T(8,128)(2,1)S(1)}, bf16[1,64,512]{2,1,0:T(8,128)(2,1)S(1)}, u32[]{:S(2)}, u32[]{:S(2)}) collective-permute-start(bf16[1,64,512]{2,1,0:T(8,128)(2,1)S(1)} %get-tuple-element.49), channel_id=1, source_target_pairs={{1,0},{2,1},{3,2},{4,3},{5,4},{6,5},{7,6},{8,7},{9,8},{10,9},{11,1... | collective-permute-start | bytes 196616 | tf_op jit(solution)/shard_map/ppermute | solution.py:20
  153.3 1.5 copy-start.27
  162.2 1.0 copy-start.15
  162.5 2.3 copy-start.24
  163.2 1.6 copy-start.7
  163.2 1.9 copy-start.8
  165.1 1.4 copy-start.21
  166.5 0.8 copy-start.18
  166.5 1.4 copy-start.11
  169.4 4.2 %copy-start.9 = (f32[1,512,512]{2,1,0:T(8,128)S(1)}, f32[1,512,512]{2,1,0:T(8,128)}, u32[]{:S(2)}) copy-start(f32[1,512,512]{2,1,0:T(8,128)} %convolution_bitcast_fusion) | copy-start | bytes 3145732
  176.5 4.2 %copy-start.17 = (bf16[512,512]{1,0:T(8,128)(2,1)S(1)}, bf16[512,512]{1,0:T(8,128)(2,1)}, u32[]{:S(2)}) copy-start(bf16[512,512]{1,0:T(8,128)(2,1)} %get-tuple-element.41) | copy-start | bytes 1572868
  180.7 1.2 copy-start.10
  187.6 1.0 copy-start.19
  190.1 34.6 %copy-start.33 = (u32[32]{0:T(128)S(1)}, u32[32]{0:T(128)}, u32[]{:S(2)}) copy-start(u32[32]{0:T(128)} %constant.40) | copy-start | bytes 388
  190.2 35.8 %copy-start.4 = (bf16[1,640,512]{2,1,0:T(8,128)(2,1)S(1)}, bf16[1,640,512]{2,1,0:T(8,128)(2,1)}, u32[]{:S(2)}) copy-start(bf16[1,640,512]{2,1,0:T(8,128)(2,1)} %copy-done.3) | copy-start | bytes 1966084
  221.2 26.6 %all-to-all-start.7 = ((bf16[16,32,512]{2,1,0:T(8,128)(2,1)}), bf16[16,32,512]{2,1,0:T(8,128)(2,1)S(1)}, u32[]{:S(2)}, u32[]{:S(2)}) async-start(bf16[16,32,512]{2,1,0:T(8,128)(2,1)} %rev.21), calls=%async_computation.7 | async-start | bytes 1048576 | tf_op jit(solution)/shard_map/all_to_all | solution.py:51
  228.2 3.5 collective-permute-start.6
  230.4 4.3 %collective-permute-start.7 = (bf16[1,64,512]{2,1,0:T(8,128)(2,1)S(1)}, bf16[1,64,512]{2,1,0:T(8,128)(2,1)S(1)}, u32[]{:S(2)}, u32[]{:S(2)}) collective-permute-start(bf16[1,64,512]{2,1,0:T(8,128)(2,1)S(1)} %get-tuple-element.45), channel_id=1, source_target_pairs={{1,0},{2,1},{3,2},{4,3},{5,4},{6,5},{7,6},{8,7},{9,8},{10,9},{11,1... | collective-permute-start | bytes 196616 | tf_op jit(solution)/shard_map/ppermute | solution.py:20
  247.8 1.2 copy-start.30
Sparse Core Ops, SparseCore 0:
  187.7 164.4 all-reduce.6
where the time goes:
time: 366 us; the launch traced here: 363 us
  blocking collectives  133 us (36%)
  waiting for transfers between devices  82.9 us (23%)
  local copies, waits for them, and re-layouts  46.2 us (13%)
  starting transfers between devices  36.5 us (10%)
  matrix products  30.5 us (8%)
  between operations  19.1 us (5%)
  other arithmetic  14.5 us (4%)
    all_to_all x3, blocking collectives, mirror(): lax.all_to_all(pieces, 'seq', split_axis=0, concat_axis=0, tiled=True)  74.9 us
    psum x1, blocking collectives, per_device(): lax.psum((jnp.stack(tap_list[::-1]), jnp.stack(gain_list[::-1]), embed_te...  58.4 us
    unnamed x2, waiting for transfers between devices  43.4 us
    all_to_all x5, waiting for transfers between devices, mirror(): lax.all_to_all(pieces, 'seq', split_axis=0, concat_axis=0, tiled=True)  36.2 us
    all_to_all x5, starting transfers between devices, mirror(): lax.all_to_all(pieces, 'seq', split_axis=0, concat_axis=0, tiled=True)  22.1 us
    another operation x4, local copies, waits for them, and re-layouts  14.7 us
    unnamed x75, local copies, waits for them, and re-layouts  13.1 us
    dot_general x7, matrix products, contract_rows(): lax.dot_general(former, latter, (((0,), (0,)), ((), ())), preferred_eleme...  9.99 us
  transfers between devices with their start and end apart: 14, of which 8 were waited for; matrix products, arithmetic and copies ran while one was open for 7% of the time, Pallas kernels for 0%

commit v1 on v0

v1 whole, which is shorter than its diff:
```python
import functools

import jax
import jax.numpy as jnp
from jax import lax
from jax.experimental import pallas as pl
from jax.experimental.pallas import tpu as pltpu
from jax.sharding import PartitionSpec as P

DMAX = 64
EPSILON = 1e-06
F32 = jnp.float32
BF16 = jnp.bfloat16


def reduce_kernel(n, steps, m0, m1, m2, m3, small, out, small_out, acc, send, recv, ssend, srecv, sems):
    me = lax.axis_index("seq")
    width = m0.shape[0] // n
    bits = [lax.rem(lax.div(me, 1 << j), 2) for j in range(steps)]
    partners = [me + (1 - 2 * bits[j]) * (1 << j) for j in range(steps)]

    barrier = pltpu.get_barrier_semaphore()
    for j in range(steps):
        pl.semaphore_signal(
            barrier, inc=1, device_id={"seq": partners[j]}, device_id_type=pl.DeviceIdType.MESH
        )

    def whole_block(dest):
        rows = pl.ds(pl.multiple_of(dest * width, width), width)
        return jnp.concatenate([m[rows, :] for m in (m0, m1, m2, m3)], axis=0)

    small_out[...] = small[...]
    base = 0
    for j in range(steps):
        count = n >> (j + 1)
        bit = bits[j]

        def pack(q, carry, j=j, base=base, bit=bit):
            at = 2 * q + (1 - bit)
            block = whole_block(at) if j == 0 else acc[at]
            send[base + q] = block.astype(BF16)
            return carry

        lax.fori_loop(0, count, pack, 0)
        ssend[j] = small_out[...]
        if j == 0:
            pl.semaphore_wait(barrier, steps)
        big = pltpu.make_async_remote_copy(
            src_ref=send.at[pl.ds(base, count)],
            dst_ref=recv.at[pl.ds(base, count)],
            send_sem=sems.at[0, j],
            recv_sem=sems.at[1, j],
            device_id={"seq": partners[j]},
            device_id_type=pl.DeviceIdType.MESH,
        )
        little = pltpu.make_async_remote_copy(
            src_ref=ssend.at[j],
            dst_ref=srecv.at[j],
            send_sem=sems.at[2, j],
            recv_sem=sems.at[3, j],
            device_id={"seq": partners[j]},
            device_id_type=pl.DeviceIdType.MESH,
        )
        big.start()
        little.start()
        big.wait()
        little.wait()

        def fold(q, carry, j=j, base=base, bit=bit):
            at = 2 * q + bit
            block = whole_block(at) if j == 0 else acc[at]
            acc[q] = block + recv[base + q].astype(F32)
            return carry

        lax.fori_loop(0, count, fold, 0)
        small_out[...] = small_out[...] + srecv[j]
        base += count
    out[...] = acc[0]


def reduce_all(mats, small):
    n = lax.axis_size("seq")
    steps = n.bit_length() - 1
    width = mats[0].shape[0] // n
    cols = mats[0].shape[1]
    vmem = pl.BlockSpec(memory_space=pltpu.VMEM)
    return pl.pallas_call(
        functools.partial(reduce_kernel, n, steps),
        out_shape=(
            jax.ShapeDtypeStruct((4 * width, cols), F32),
            jax.ShapeDtypeStruct(small.shape, F32),
        ),
        in_specs=[vmem] * 5,
        out_specs=(vmem, vmem),
        scratch_shapes=[
            pltpu.VMEM((n // 2, 4 * width, cols), F32),
            pltpu.VMEM((n - 1, 4 * width, cols), BF16),
            pltpu.VMEM((n - 1, 4 * width, cols), BF16),
            pltpu.VMEM((steps,) + small.shape, F32),
            pltpu.VMEM((steps,) + small.shape, F32),
            pltpu.SemaphoreType.DMA((4, steps)),
        ],
        compiler_params=pltpu.CompilerParams(
            collective_id=0, has_side_effects=True, vmem_limit_bytes=48 * 1024 * 1024
        ),
    )(*mats, small)


def dot(a, b):
    return lax.dot_general(a, b, (((a.ndim - 1,), (0,)), ((), ())), preferred_element_type=F32)


def dot_t(a, b):
    return lax.dot_general(a, b, (((a.ndim - 1,), (1,)), ((), ())), preferred_element_type=F32)


def over_rows(a, b):
    return lax.dot_general(
        a.reshape(-1, a.shape[-1]),
        b.reshape(-1, b.shape[-1]),
        (((0,), (0,)), ((), ())),
        preferred_element_type=F32,
    )


def parts(a):
    high = a.astype(BF16)
    return high, (a - high.astype(F32)).astype(BF16)


def table_dot(table, w, transposed=False):
    high, low = parts(table)
    both = jnp.concatenate([high, low], axis=0)
    product = dot_t(both, w) if transposed else dot(both, w)
    return product[: table.shape[0]] + product[table.shape[0] :]


def look_up(hot, table):
    high, low = parts(table)
    return dot(jnp.concatenate([hot, hot], axis=-1), jnp.concatenate([high, low], axis=0))


def windows(rows, start, count, dilation):
    out = []
    for k in range(3):
        first = lax.dynamic_slice_in_dim(rows[0], start + (k - 1) * dilation, count, 0)
        second = lax.dynamic_slice_in_dim(rows[1], start - (k - 1) * dilation, count, 0)
        out.append(jnp.stack([first, second]))
    return out


def flipped(rows):
    size = rows.shape[0]
    at = lax.broadcasted_iota(jnp.int32, (size, size), 0)
    to = lax.broadcasted_iota(jnp.int32, (size, size), 1)
    return dot((at + to == size - 1).astype(BF16), rows).astype(BF16)


def per_device(tokens, dilations, embedding, norm_gain, conv_taps, w_up, w_gate, w_out, cotangent):
    n = lax.axis_size("seq")
    me = lax.axis_index("seq")
    rows = tokens.shape[0]
    half = rows // 2
    channels = embedding.shape[1]
    to_mirror = [(i, n - 1 - i) for i in range(n)]
    to_next = [(i, (i + 1) % n) for i in range(n)]
    to_beyond = [(i, (n - i) % n) for i in range(n)]

    tok_prev = lax.ppermute(tokens, "seq", to_next)
    tok_mirror = lax.ppermute(tokens, "seq", to_mirror)
    tok_beyond = lax.ppermute(tokens, "seq", to_beyond)
    cot_mirror = lax.ppermute(cotangent[half - DMAX :], "seq", to_mirror)
    cot_prev = lax.ppermute(cotangent[rows - DMAX :], "seq", to_next)
    cot_beyond = lax.ppermute(cotangent[:DMAX], "seq", to_beyond)

    edge = 3 * DMAX
    tok = jnp.stack(
        [
            jnp.concatenate([tok_prev[rows - edge :], tokens[: half + edge]]),
            jnp.flip(jnp.concatenate([tok_mirror[half - edge :], tok_beyond[:edge]])),
        ]
    )
    position = me * rows - edge + jnp.arange(half + 2 * edge, dtype=jnp.int32)
    inside = position >= 0
    bases = jnp.arange(4, dtype=jnp.int32)
    hot = ((tok[:, :, None] == bases) & inside[None, :, None]).astype(BF16)

    wide0 = embedding.astype(F32)
    inverse0 = lax.rsqrt(jnp.mean(wide0 * wide0, axis=-1, keepdims=True) + EPSILON)
    unit0 = wide0 * inverse0
    table = (unit0 * norm_gain[0]).astype(BF16)
    table_wide = table.astype(F32)
    tapped = (conv_taps[0][:, None, :] * table_wide[None]).reshape(12, channels)
    up_table = table_dot(tapped, w_up[0])
    gate_table = jax.nn.sigmoid(dot(table, w_gate[0]))

    d0, d1 = dilations[0], dilations[1]
    count1 = half + 4 * DMAX
    hot12 = jnp.concatenate(windows(hot, DMAX, count1, d0), axis=-1)
    hot_own = hot[:, DMAX : DMAX + count1]
    hot_partner = hot_own[::-1]
    upward0 = look_up(hot12, up_table)
    gate0 = look_up(hot_partner, gate_table)
    hidden0 = (upward0 * gate0).astype(BF16)
    wide = (dot(hot_own, embedding) + dot(hidden0, w_out[0])).astype(BF16).astype(F32)

    inverse = lax.rsqrt(jnp.mean(wide * wide, axis=-1, keepdims=True) + EPSILON)
    unit = wide * inverse
    normed = jnp.where(
        inside[None, DMAX : DMAX + count1, None], unit * norm_gain[1], 0.0
    ).astype(BF16)

    taps1 = conv_taps[1]
    count2 = half + 2 * DMAX
    shifted = windows(normed, DMAX, count2, d1)
    mixed = sum(taps1[k] * shifted[k].astype(F32) for k in range(3)).astype(BF16)
    partner = normed[::-1, DMAX : DMAX + count2]
    upward = dot(mixed, w_up[1])
    gate = jax.nn.sigmoid(dot(partner, w_gate[1]))
    hidden = (upward * gate).astype(BF16)

    cot_first = jnp.concatenate([cot_prev, cotangent[: half + DMAX]])
    cot_second = flipped(jnp.concatenate([cot_mirror, cot_beyond]))
    low = jnp.where(
        inside[None, 2 * DMAX : 2 * DMAX + count2, None],
        jnp.stack([cot_first, cot_second]),
        jnp.zeros((), BF16),
    )
    grad_hidden = dot_t(low, w_out[1])
    grad_upward = (grad_hidden * gate).astype(BF16)
    grad_logit = (grad_hidden * upward * gate * (1.0 - gate)).astype(BF16)
    own = slice(DMAX, DMAX + half)
    term_out1 = over_rows(low[:, own], hidden[:, own])
    term_up1 = over_rows(grad_upward[:, own], mixed[:, own])
    term_gate1 = over_rows(grad_logit[:, own], partner[:, own])
    grad_mixed = dot_t(grad_upward, w_up[1]).astype(BF16)
    grad_partner = dot_t(grad_logit[:, own], w_gate[1]).astype(BF16)

    moved = windows(grad_mixed, DMAX, half, -d1)
    grad_normed = sum(taps1[k] * moved[k].astype(F32) for k in range(3))
    grad_normed = grad_normed + grad_partner[::-1].astype(F32)
    mixed_own = grad_mixed[:, own].astype(F32)
    taps_term = jnp.stack(
        [jnp.sum(mixed_own * shifted[k][:, own].astype(F32), axis=(0, 1)) for k in range(3)]
    )
    unit_own = unit[:, 2 * DMAX : 2 * DMAX + half]
    inverse_own = inverse[:, 2 * DMAX : 2 * DMAX + half]
    gain_term = jnp.sum(grad_normed * unit_own, axis=(0, 1))[None]
    grad_unit = grad_normed * norm_gain[1]
    gradient = low[:, own].astype(F32) + inverse_own * (
        grad_unit - unit_own * jnp.mean(grad_unit * unit_own, axis=-1, keepdims=True)
    )

    low0, rest0 = parts(gradient)
    own0 = slice(2 * DMAX, 2 * DMAX + half)
    grad_hidden0 = dot_t(low0, w_out[0])
    gate_own = gate0[:, own0]
    grad_upward0 = grad_hidden0 * gate_own
    grad_logit0 = (grad_upward0 * upward0[:, own0] * (1.0 - gate_own)).astype(BF16)
    term_out0 = over_rows(low0, hidden0[:, own0])
    sum_up = over_rows(hot12[:, own0], grad_upward0.astype(BF16))
    sum_logit = over_rows(hot_partner[:, own0], grad_logit0)
    hot_here = hot_own[:, own0]
    sum_grad = over_rows(hot_here, low0) + over_rows(hot_here, rest0)

    small = jnp.concatenate([sum_up, sum_logit, sum_grad, taps_term, gain_term], axis=0)
    mats, small = reduce_all((term_out0, term_out1, term_up1, term_gate1), small)

    width = channels // n
    sum_up, sum_logit, sum_grad = small[:12], small[12:16], small[16:20]
    columns = jnp.concatenate([sum_up, sum_logit], axis=0)
    mine = lax.dynamic_slice_in_dim(columns, me * width, width, 1)
    exact = functools.partial(
        lax.dot_general,
        dimension_numbers=(((0,), (0,)), ((), ())),
        precision=lax.Precision.HIGHEST,
        preferred_element_type=F32,
    )
    out0, out1, up1, gate1 = [m.T for m in mats.reshape(4, width, channels)]
    grad_up = jnp.stack([exact(tapped, mine[:12]), up1])
    grad_gate = jnp.stack([exact(table_wide, mine[12:]), gate1])
    grad_out = jnp.stack([out0, out1])

    spread = table_dot(sum_up, w_up[0], True).reshape(3, 4, channels)
    grad_normed0 = jnp.sum(conv_taps[0][:, None, :] * spread, axis=0)
    grad_normed0 = grad_normed0 + table_dot(sum_logit, w_gate[0], True)
    grad_taps = jnp.stack([jnp.sum(spread * table_wide[None], axis=1), small[20:23]])
    grad_gain = jnp.stack([jnp.sum(grad_normed0 * unit0, axis=0), small[23]])
    grad_unit0 = grad_normed0 * norm_gain[0]
    grad_embed = sum_grad + inverse0 * (
        grad_unit0 - unit0 * jnp.mean(grad_unit0 * unit0, axis=-1, keepdims=True)
    )
    return (grad_up, grad_gate, grad_out, grad_taps, grad_gain, grad_embed)


def solution(mesh):
    in_specs = (P(("groups", "seq")), P(), P(), P(), P(), P(), P(), P(), P(("groups", "seq"), None))
    out_specs = (
        P("groups", None, "seq"),
        P("groups", None, "seq"),
        P("groups", None, "seq"),
        P("groups", None, None),
        P("groups", None),
        P("groups", None),
    )
    return jax.shard_map(
        per_device, mesh=mesh, in_specs=in_specs, out_specs=out_specs, check_vma=False
    )
```

time: 366 us -> 118 us (0.32)
  blocking collectives: 133 us -> 0 us
  waiting for transfers between devices: 82.9 us -> 0.02 us
  Pallas kernels: 0 us -> 36.1 us
  starting transfers between devices: 36.5 us -> 16.8 us
  local copies, waits for them, and re-layouts: 46.2 us -> 26.6 us
  matrix products: 30.5 us -> 18 us
  between operations: 19.1 us -> 8.73 us
  other arithmetic: 14.5 us -> 10.3 us
    all_to_all x3 -> x0, blocking collectives: 74.9 us -> none  [mirror(): lax.all_to_all(pieces, 'seq', split_axis=0, concat_axis=0, tiled=True)]
    psum x1 -> x0, blocking collectives: 58.4 us -> none  [per_device(): lax.psum((jnp.stack(tap_list[::-1]), jnp.stack(gain_list[::-1]), embed_te...]
    unnamed x2 -> x0, waiting for transfers between devices: 43.4 us -> none
    all_to_all x5 -> x0, waiting for transfers between devices: 36.2 us -> none  [mirror(): lax.all_to_all(pieces, 'seq', split_axis=0, concat_axis=0, tiled=True)]
    pallas_call x0 -> x1, Pallas kernels: none -> 36.1 us  [reduce_all(): pl.pallas_call(functools.partial(reduce_kernel, n, steps), out_shape=(jax...]
    another operation x7 -> x5, local copies, waits for them, and re-layouts: 27.2 us -> 0.11 us  [the longest x1 0.08 us: windows(): out.append(jnp.stack([first, second]))]
    all_to_all x5 -> x0, starting transfers between devices: 22.1 us -> none  [mirror(): lax.all_to_all(pieces, 'seq', split_axis=0, concat_axis=0, tiled=True)]
    dot_general x19 -> x25, matrix products: 30.5 us -> 18 us  [the longest x9 10.7 us: dot(): lax.dot_general(a, b, (((a.ndim - 1,), (0,)), ((), ())), preferred_elemen...]
  transfers between devices with their start and end apart: 14 -> 6, of which waited for: 8 -> 0; matrix products, arithmetic and copies ran while one was open for 7% -> 25% of each run, Pallas kernels for 0% -> 0%
where the time goes in v1:
time: 118 us; the launch traced here: 117 us
  Pallas kernels  36.1 us (31%)
  local copies, waits for them, and re-layouts  26.6 us (23%)
  matrix products  18 us (15%)
  starting transfers between devices  16.8 us (14%)
  other arithmetic  10.3 us (9%)
  between operations  8.73 us (7%)
    pallas_call x1, Pallas kernels, reduce_all(): pl.pallas_call(functools.partial(reduce_kernel, n, steps), out_shape=(jax...  36.1 us
    unnamed x124, local copies, waits for them, and re-layouts  10.7 us
    dot_general x9, matrix products, dot(): lax.dot_general(a, b, (((a.ndim - 1,), (0,)), ((), ())), preferred_elemen...  10.7 us
    ppermute x1, starting transfers between devices, per_device(): tok_mirror = lax.ppermute(tokens, 'seq', to_mirror)  7.19 us
    ppermute x1, starting transfers between devices, per_device(): cot_mirror = lax.ppermute(cotangent[half - DMAX:], 'seq', to_mirror)  5.42 us
    dot_general x8, matrix products, over_rows(): lax.dot_general(a.reshape(-1, a.shape[-1]), b.reshape(-1, b.shape[-1]), (...  4.06 us
    slice x2, local copies, waits for them, and re-layouts, per_device(): term_gate1 = over_rows(grad_logit[:, own], partner[:, own])  2.73 us
    dot_general x6, matrix products, dot_t(): lax.dot_general(a, b, (((a.ndim - 1,), (1,)), ((), ())), preferred_elemen...  2.61 us
  transfers between devices with their start and end apart: 6, of which 0 were waited for; matrix products, arithmetic and copies ran while one was open for 25% of the time, Pallas kernels for 0%

profile of v1, /device:TPU:0, one launch (start us, length us, event | category | flops | bytes accessed | tf_op | source)
XLA Modules:
  0.0 116.6 jit_solution(6563956981988965804)
XLA Ops:
  0.7 0.5 collective-permute-start.3
  1.2 1.5 %collective-permute-start.5 = (s32[512]{0:T(512)}, s32[512]{0:T(512)S(1)}, u32[]{:S(2)}, u32[]{:S(2)}) collective-permute-start(s32[512]{0:T(512)} %param.9), channel_id=1, source_target_pairs={{0,0},{1,15},{2,14},{3,13},{4,12},{5,11},{6,10},{7,9},{8,8},{9,7},... | collective-permute-start | bytes 6152 | tf_op jit(solution)/shard_map/ppermute | solution.py:171
  2.7 7.2 %collective-permute-start.4 = (s32[512]{0:T(512)}, s32[512]{0:T(512)S(1)}, u32[]{:S(2)}, u32[]{:S(2)}) collective-permute-start(s32[512]{0:T(512)} %param.9), channel_id=1, source_target_pairs={{0,15},{1,14},{2,13},{3,12},{4,11},{5,10},{6,9},{7,8},{8,7},{9,6},... | collective-permute-start | bytes 6152 | tf_op jit(solution)/shard_map/ppermute | solution.py:170
  9.8 1.5 %fusion.121 = (bf16[64,512]{1,0:T(8,128)(2,1)}, bf16[64,512]{1,0:T(8,128)(2,1)}) fusion(bf16[512,512]{1,0:T(8,128)(2,1)} %param.17), kind=kLoop, calls=%fused_computation.211 | loop fusion | bytes 262144 | tf_op jit(solution)/shard_map/slice | solution.py:173
  11.4 2.2 %collective-permute-start.2 = (bf16[64,512]{1,0:T(8,128)(2,1)}, bf16[64,512]{1,0:T(8,128)(2,1)}, u32[]{:S(2)}, u32[]{:S(2)}) collective-permute-start(bf16[64,512]{1,0:T(8,128)(2,1)} %get-tuple-element.59), channel_id=1, source_target_pairs={{0,0},{1,15},{2,14},{3,13},{4,12},{5,11},{6,10},{7,9},{8,8},{9,7},... | collective-permute-start | bytes 196616 | tf_op jit(solution)/shard_map/ppermute | solution.py:174
  13.7 0.6 slice.249
  14.3 1.3 %fusion.126 = (s32[1]{0:T(128)}, s32[1]{0:T(128)}) fusion(s32[2]{0:T(128)} %param.10), kind=kLoop, calls=%fused_computation.216 | loop fusion | bytes 16 | tf_op jit(solution)/shard_map/slice | solution.py:197
  22.7 1.3 %fusion.123 = (f32[1,1,512]{2,0,1:T(1,128)}, f32[1,1,512]{2,0,1:T(1,128)}, f32[1,1,512]{2,0,1:T(1,128)}) fusion(f32[2,3,512]{2,0,1:T(2,128)} %param.13), kind=kLoop, calls=%fused_computation.213 | loop fusion | bytes 12288 | tf_op jit(solution)/shard_map/slice | solution.py:240
  24.0 2.0 %fusion.122 = (bf16[320,512]{1,0:T(8,128)(2,1)}, bf16[320,512]{1,0:T(8,128)(2,1)}) fusion(bf16[512,512]{1,0:T(8,128)(2,1)} %param.17), kind=kLoop, calls=%fused_computation.212 | loop fusion | bytes 1310720 | tf_op jit(solution)/shard_map/slice | solution.py:222
  26.9 5.4 %collective-permute-start.1 = (bf16[320,512]{1,0:T(8,128)(2,1)}, bf16[320,512]{1,0:T(8,128)(2,1)}, u32[]{:S(2)}, u32[]{:S(2)}) collective-permute-start(bf16[320,512]{1,0:T(8,128)(2,1)} %get-tuple-element.61), channel_id=1, source_target_pairs={{0,15},{1,14},{2,13},{3,12},{4,11},{5,10},{6,9},{7,8},{8,7},{9,6},... | collective-permute-start | bytes 983048 | tf_op jit(solution)/shard_map/ppermute | solution.py:172
  33.4 0.6 fusion.74
  34.3 0.5 copy-done.31
  35.4 1.8 %multiply_convert_fusion = (bf16[2,512,512]{2,1,0:T(8,128)(2,1)S(1)}, f32[2,512,512]{2,1,0:T(8,128)}) fusion(f32[2,512,512]{2,1,0:T(8,128)S(1)} %fusion.70, bf16[2,512,24]{1,2,0:T(8,128)(2,1)S(1)} %concatenate.47, bf16[12,512]{1,0:T(8,128)(2,1)S(1)} %get-tuple-element.39, bf16[12,512]{1,0:T(8,128)(2,1)S(1)} %get-tuple-element.40), kind=kOutput, calls=%fused_computation.5 | convolution fusion | flops 26263552 | bytes 5316608 | tf_op jit(solution)/shard_map/dot_general | solution.py:110
  37.4 0.8 fusion
  38.2 0.6 fusion.109
  38.8 1.8 %select_convert_fusion = (bf16[2,512,512]{2,1,0:T(8,128)(2,1)S(1)}, f32[2,512,512]{2,1,0:T(8,128)}) fusion(f32[512]{0:T(512)S(1)} %bitcast.152, pred[512]{0:T(512)(128)(4,1)S(1)} %slice.271, f32[2,512]{1,0:T(2,128)S(1)} %get-tuple-element.80, bf16[2,512,512]{2,1,0:T(8,128)(2,1)S(1)} %get-tuple-element.88), kind=kLoop, calls=%fused_computation.3 | loop fusion | flops 2621440 | bytes 4200960 | tf_op jit(solution)/shard_map/convert_element_type | solution.py:211
  40.6 0.9 slice.317
  41.6 2.1 %rev.15 = bf16[2,384,512]{2,1,0:T(8,128)(2,1)} reverse(bf16[2,384,512]{2,1,0:T(8,128)(2,1)} %slice.317), dimensions={0} | reverse | bytes 1572864 | tf_op jit(solution)/shard_map/rev | solution.py:217
  43.7 3.3 %add_divide_fusion = f32[2,384,512]{2,1,0:T(8,128)} fusion(bf16[2,384,512]{2,1,0:T(8,128)(2,1)} %rev.15, bf16[2,512,512]{2,1,0:T(8,128)(2,1)} %param.15), kind=kOutput, calls=%fused_computation.12 | convolution fusion | flops 403832832 | bytes 2883584 | tf_op jit(solution)/shard_map/dot_general | solution.py:110
  48.3 0.6 copy-done.14
  48.9 1.7 %fusion.22 = f32[2,384,512]{2,1,0:T(8,128)} fusion(bf16[2,384,512]{2,1,0:T(8,128)(2,1)S(1)} %add_convert_fusion.1, bf16[2,512,512]{2,1,0:T(8,128)(2,1)S(1)} %copy-done.14), kind=kOutput, calls=%fused_computation.64 | convolution fusion | flops 402653184 | bytes 2883584 | tf_op jit(solution)/shard_map/dot_general | solution.py:110
  50.7 0.6 slice_bitcast_fusion.5
  51.3 0.8 slice.333
  52.0 0.8 slice.331
  52.9 0.6 slice.294
  53.5 1.9 %slice.290 = bf16[2,256,512]{2,1,0:T(8,128)(2,1)} reverse(bf16[2,256,512]{2,1,0:T(8,128)(2,1)} %slice.331), dimensions={0} | reverse | bytes 1048576 | tf_op jit(solution)/shard_map/slice | solution.py:235
  55.4 1.0 maximum_bitcast_fusion
  56.4 1.5 %fusion.1 = bf16[1,384,512]{2,1,0:T(8,128)(2,1)S(1)} fusion(bf16[64,512]{1,0:T(8,128)(2,1)} %collective-permute-done.2, bf16[320,512]{1,0:T(8,128)(2,1)} %collective-permute-done.1), kind=kOutput, calls=%fused_computation.21 | convolution fusion | flops 152272896 | bytes 786432 | tf_op jit(solution)/shard_map/dot_general | solution.py:110
  58.2 0.6 multiply_convert_fusion.1
  58.8 1.5 %convolution_bitcast_fusion.1.m2 = f32[512,512]{1,0:T(8,128)} fusion(bf16[2,384,512]{2,1,0:T(8,128)(2,1)S(1)} %add_convert_fusion.1, bf16[2,384,512]{2,1,0:T(8,128)(2,1)S(1)} %get-tuple-element.89), kind=kOutput, calls=%fused_computation.16 | convolution fusion | flops 268435456 | bytes 2097152 | tf_op jit(solution)/shard_map/dot_general | solution.py:118
  60.3 0.6 convolution_convert_fusion
  60.9 0.8 copy-done.5
  61.7 0.5 convolution_bitcast_fusion.2.m1
  62.6 0.8 copy-done.23
  64.3 1.2 %copy-done.3 = f32[2,512,512]{2,1,0:T(8,128)S(1)} copy-done((f32[2,512,512]{2,1,0:T(8,128)S(1)}, f32[2,512,512]{2,1,0:T(8,128)}, u32[]{:S(2)}) %copy-start.3) | copy-done | bytes 2097176
  65.8 1.6 %fusion.11 = (f32[512]{0:T(512)}, f32[512]{0:T(512)}, f32[512]{0:T(512)}, f32[2,256]{1,0:T(2,128)S(1)}, f32[512]{0:T(512)}, /*index=5*/f32[2,256,512]{2,1,0:T(8,128)S(1)}) fusion(bf16[1,384,512]{2,1,0:T(8,128)(2,1)S(1)} %copy-done.8, bf16[1,384,512]{2,1,0:T(8,128)(2,1)S(1)} %copy-done.12, bf16[2,384,512]{2,1,0:T(8,128)(2,1)S(1)} %convolution_convert_fusion, ...), kind=kLoop, calls=%fused_computation.38 | loop fusion | flops 9434624 | bytes 6309888 | tf_op jit(solution)/shard_map/reduce_sum | solution.py:244
  68.1 0.5 convolution_bitcast_fusion.7
  69.1 1.1 copy-done.2
  70.6 0.6 copy-done.19
  72.1 0.7 copy-done.6
  73.6 1.2 %copy-done = f32[512,512]{1,0:T(8,128)S(1)} copy-done((f32[512,512]{1,0:T(8,128)S(1)}, f32[512,512]{1,0:T(8,128)}, u32[]{:S(2)}) %copy-start) | copy-done | bytes 1048600
  74.8 36.1 %shard_map.136 = (f32[128,512]{1,0:T(8,128)S(1)}, f32[24,512]{1,0:T(8,128)S(1)}) custom-call(f32[512,512]{1,0:T(8,128)S(1)} %convolution_bitcast_fusion.3.m0, f32[512,512]{1,0:T(8,128)S(1)} %convolution_bitcast_fusion.2.m1, f32[512,512]{1,0:T(8,128)S(1)} %copy-done, f32[512,512]{1,0:T(8,128)S(1)} %convolution_bitcast_fusion.m3, f32[24,512]{1,0:T(8,128)S(1)} %concatenate.53.small), custom_call_target="tpu_custom_call" | custom-call | tf_op jit(solution)/shard_map/pallas_call | solution.py:87
  112.7 0.6 copy.24
  113.3 0.7 pad_maximum_fusion.4
  114.0 0.7 pad_maximum_fusion.2
  114.6 0.7 pad_maximum_fusion.3
  115.3 0.7 fusion.86
  116.0 0.6 pad_maximum_fusion.13
  (188 shorter events, 10.7 us)
Async XLA Ops:
  0.6 25.6 %slice-start = ((f32[2,3,512]{2,0,1:T(2,128)}), f32[1,3,512]{2,0,1:T(1,128)S(1)}, s32[]{:S(2)}) async-start(f32[2,3,512]{2,0,1:T(2,128)} %param.13), calls=%async_computation | async-start | bytes 12288 | tf_op jit(solution)/shard_map/slice | solution.py:193
  0.6 25.4 %copy-start.26 = (bf16[4,512]{1,0:T(4,128)(2,1)S(1)}, bf16[4,512]{1,0:T(4,128)(2,1)}, u32[]{:S(2)}) copy-start(bf16[4,512]{1,0:T(4,128)(2,1)} %param.11) | copy-start | bytes 12292
  0.7 25.5 %copy-start.58 = (f32[2,512]{1,0:T(2,128)S(1)}, f32[2,512]{1,0:T(2,128)}, u32[]{:S(2)}) copy-start(f32[2,512]{1,0:T(2,128)} %param.12) | copy-start | bytes 12292
  0.7 25.7 %copy-start.22 = (bf16[2,512,512]{2,1,0:T(8,128)(2,1)S(1)}, bf16[2,512,512]{2,1,0:T(8,128)(2,1)}, u32[]{:S(2)}) copy-start(bf16[2,512,512]{2,1,0:T(8,128)(2,1)} %param.15) | copy-start | bytes 3145732
  0.7 26.0 %copy-start.13 = (bf16[2,512,512]{2,1,0:T(8,128)(2,1)S(1)}, bf16[2,512,512]{2,1,0:T(8,128)(2,1)}, u32[]{:S(2)}) copy-start(bf16[2,512,512]{2,1,0:T(8,128)(2,1)} %param.14) | copy-start | bytes 3145732
  0.7 26.2 %collective-permute-start.3 = (s32[512]{0:T(512)}, s32[512]{0:T(512)S(1)}, u32[]{:S(2)}, u32[]{:S(2)}) collective-permute-start(s32[512]{0:T(512)} %param.9), channel_id=1, source_target_pairs={{0,1},{1,2},{2,3},{3,4},{4,5},{5,6},{6,7},{7,8},{8,9},{9,10},{10,1... | collective-permute-start | bytes 6152 | tf_op jit(solution)/shard_map/ppermute | solution.py:169
  1.2 31.3 %collective-permute-start.5 = (s32[512]{0:T(512)}, s32[512]{0:T(512)S(1)}, u32[]{:S(2)}, u32[]{:S(2)}) collective-permute-start(s32[512]{0:T(512)} %param.9), channel_id=1, source_target_pairs={{0,0},{1,15},{2,14},{3,13},{4,12},{5,11},{6,10},{7,9},{8,8},{9,7},... | collective-permute-start | bytes 6152 | tf_op jit(solution)/shard_map/ppermute | solution.py:171
  2.7 29.9 %collective-permute-start.4 = (s32[512]{0:T(512)}, s32[512]{0:T(512)S(1)}, u32[]{:S(2)}, u32[]{:S(2)}) collective-permute-start(s32[512]{0:T(512)} %param.9), channel_id=1, source_target_pairs={{0,15},{1,14},{2,13},{3,12},{4,11},{5,10},{6,9},{7,8},{8,7},{9,6},... | collective-permute-start | bytes 6152 | tf_op jit(solution)/shard_map/ppermute | solution.py:170
  11.4 21.1 %copy-start.59 = (s32[512]{0:T(512)S(1)}, s32[512]{0:T(512)}, u32[]{:S(2)}) copy-start(s32[512]{0:T(512)} %param.9) | copy-start | bytes 6148
  11.4 44.0 %collective-permute-start = (bf16[64,512]{1,0:T(8,128)(2,1)}, bf16[64,512]{1,0:T(8,128)(2,1)}, u32[]{:S(2)}, u32[]{:S(2)}) collective-permute-start(bf16[64,512]{1,0:T(8,128)(2,1)} %get-tuple-element.58), channel_id=1, source_target_pairs={{0,1},{1,2},{2,3},{3,4},{4,5},{5,6},{6,7},{7,8},{8,9},{9,10},{10,1... | collective-permute-start | bytes 196616 | tf_op jit(solution)/shard_map/ppermute | solution.py:173
  11.4 45.0 %collective-permute-start.2 = (bf16[64,512]{1,0:T(8,128)(2,1)}, bf16[64,512]{1,0:T(8,128)(2,1)}, u32[]{:S(2)}, u32[]{:S(2)}) collective-permute-start(bf16[64,512]{1,0:T(8,128)(2,1)} %get-tuple-element.59), channel_id=1, source_target_pairs={{0,0},{1,15},{2,14},{3,13},{4,12},{5,11},{6,10},{7,9},{8,8},{9,7},... | collective-permute-start | bytes 196616 | tf_op jit(solution)/shard_map/ppermute | solution.py:174
  26.2 7.9 %copy-start.56 = (f32[4]{0:T(128)}, f32[4]{0:T(128)S(1)}, u32[]{:S(2)}) copy-start(f32[4]{0:T(128)S(1)} %add_rsqrt_fusion.1) | copy-start | bytes 52
  26.2 7.8 %copy-start.41 = (f32[1,512]{1,0:T(1,128)}, f32[1,512]{1,0:T(1,128)S(1)}, u32[]{:S(2)}) copy-start(f32[1,512]{1,0:T(1,128)S(1)} %get-tuple-element.82) | copy-start | bytes 6148
  26.2 7.8 %copy-start.27 = (f32[1,3,512]{2,1,0:T(4,128)}, f32[1,3,512]{2,1,0:T(4,128)S(1)}, u32[]{:S(2)}) copy-start(f32[1,3,512]{2,1,0:T(4,128)S(1)} %copy.31) | copy-start | bytes 18436
  26.3 7.7 %copy-start.29 = (f32[4,512]{1,0:T(4,128)}, f32[4,512]{1,0:T(4,128)S(1)}, u32[]{:S(2)}) copy-start(f32[4,512]{1,0:T(4,128)S(1)} %fusion.112) | copy-start | bytes 24580
  26.6 6.3 %copy-start.20 = (f32[12,512]{1,0:T(8,128)}, f32[12,512]{1,0:T(8,128)S(1)}, u32[]{:S(2)}) copy-start(f32[12,512]{1,0:T(8,128)S(1)} %mul.252) | copy-start | bytes 73732
  26.9 29.5 %collective-permute-start.1 = (bf16[320,512]{1,0:T(8,128)(2,1)}, bf16[320,512]{1,0:T(8,128)(2,1)}, u32[]{:S(2)}, u32[]{:S(2)}) collective-permute-start(bf16[320,512]{1,0:T(8,128)(2,1)} %get-tuple-element.61), channel_id=1, source_target_pairs={{0,15},{1,14},{2,13},{3,12},{4,11},{5,10},{6,9},{7,8},{8,7},{9,6},... | collective-permute-start | bytes 983048 | tf_op jit(solution)/shard_map/ppermute | solution.py:172
  32.8 1.3 %copy-start.39 = (pred[2,640,4]{1,2,0:T(4,128)(4,1)}, pred[2,640,4]{1,2,0:T(4,128)(4,1)S(1)}, u32[]{:S(2)}) copy-start(pred[2,640,4]{1,2,0:T(4,128)(4,1)S(1)} %get-tuple-element.44) | copy-start | bytes 15364
  34.2 3.0 %copy-start.33 = (bf16[1,512,4]{1,2,0:T(4,128)(2,1)}, bf16[1,512,4]{1,2,0:T(4,128)(2,1)S(1)}, u32[]{:S(2)}) copy-start(bf16[1,512,4]{1,2,0:T(4,128)(2,1)S(1)} %get-tuple-element.78) | copy-start | bytes 12292
  34.2 3.0 %copy-start.35 = (bf16[1,512,4]{1,2,0:T(4,128)(2,1)}, bf16[1,512,4]{1,2,0:T(4,128)(2,1)S(1)}, u32[]{:S(2)}) copy-start(bf16[1,512,4]{1,2,0:T(4,128)(2,1)S(1)} %get-tuple-element.91) | copy-start | bytes 12292
  35.4 2.1 %copy-start.1 = (f32[2,512,512]{2,1,0:T(8,128)}, f32[2,512,512]{2,1,0:T(8,128)S(1)}, u32[]{:S(2)}) copy-start(f32[2,512,512]{2,1,0:T(8,128)S(1)} %fusion.70) | copy-start | bytes 6291460
  35.4 2.0 %copy-start.17 = (bf16[2,512,512]{2,1,0:T(8,128)(2,1)S(1)}, bf16[2,512,512]{2,1,0:T(8,128)(2,1)}, u32[]{:S(2)}) copy-start(bf16[2,512,512]{2,1,0:T(8,128)(2,1)} %param.16) | copy-start | bytes 3145732
  47.7 1.2 %copy-start.14 = (bf16[2,512,512]{2,1,0:T(8,128)(2,1)S(1)}, bf16[2,512,512]{2,1,0:T(8,128)(2,1)}, u32[]{:S(2)}) copy-start(bf16[2,512,512]{2,1,0:T(8,128)(2,1)} %param.14) | copy-start | bytes 3145732
  48.9 1.8 %copy-start.51 = (f32[2,512,1]{1,0,2:T(2,128)S(1)}, f32[2,512,1]{1,0,2:T(2,128)}, u32[]{:S(2)}) copy-start(f32[2,512,1]{1,0,2:T(2,128)} %get-tuple-element.79) | copy-start | bytes 12292
  52.9 5.1 %copy-start.60 = (pred[384]{0:T(512)(128)(4,1)S(1)}, pred[384]{0:T(512)(128)(4,1)}, u32[]{:S(2)}) copy-start(pred[384]{0:T(512)(128)(4,1)} %slice.249) | copy-start | bytes 1156
  56.4 1.7 %copy-start.4 = (f32[2,384,512]{2,1,0:T(8,128)S(1)}, f32[2,384,512]{2,1,0:T(8,128)}, u32[]{:S(2)}) copy-start(f32[2,384,512]{2,1,0:T(8,128)} %add_divide_fusion) | copy-start | bytes 4718596
  56.4 1.8 %copy-start.18 = (bf16[2,512,512]{2,1,0:T(8,128)(2,1)S(1)}, bf16[2,512,512]{2,1,0:T(8,128)(2,1)}, u32[]{:S(2)}) copy-start(bf16[2,512,512]{2,1,0:T(8,128)(2,1)} %param.16) | copy-start | bytes 3145732
  58.8 1.5 %copy-start.15 = (bf16[2,512,512]{2,1,0:T(8,128)(2,1)S(1)}, bf16[2,512,512]{2,1,0:T(8,128)(2,1)}, u32[]{:S(2)}) copy-start(bf16[2,512,512]{2,1,0:T(8,128)(2,1)} %param.14) | copy-start | bytes 3145732
  60.3 1.4 %copy-start.5 = (f32[2,384,512]{2,1,0:T(8,128)S(1)}, f32[2,384,512]{2,1,0:T(8,128)}, u32[]{:S(2)}) copy-start(f32[2,384,512]{2,1,0:T(8,128)} %fusion.22) | copy-start | bytes 4718596
  62.2 1.2 %copy-start.23 = (bf16[2,512,512]{2,1,0:T(8,128)(2,1)S(1)}, bf16[2,512,512]{2,1,0:T(8,128)(2,1)}, u32[]{:S(2)}) copy-start(bf16[2,512,512]{2,1,0:T(8,128)(2,1)} %param.15) | copy-start | bytes 3145732
  63.9 1.6 %copy-start.3 = (f32[2,512,512]{2,1,0:T(8,128)S(1)}, f32[2,512,512]{2,1,0:T(8,128)}, u32[]{:S(2)}) copy-start(f32[2,512,512]{2,1,0:T(8,128)} %get-tuple-element.46) | copy-start | bytes 6291460
  63.9 1.6 %copy-start.8 = (bf16[1,384,512]{2,1,0:T(8,128)(2,1)S(1)}, bf16[1,384,512]{2,1,0:T(8,128)(2,1)}, u32[]{:S(2)}) copy-start(bf16[1,384,512]{2,1,0:T(8,128)(2,1)} %copy-done.7) | copy-start | bytes 1179652
  63.9 1.7 %copy-start.10 = (bf16[1,384,512]{2,1,0:T(8,128)(2,1)S(1)}, bf16[1,384,512]{2,1,0:T(8,128)(2,1)}, u32[]{:S(2)}) copy-start(bf16[1,384,512]{2,1,0:T(8,128)(2,1)} %copy-done.9) | copy-start | bytes 1179652
  63.9 1.8 %copy-start.12 = (bf16[1,384,512]{2,1,0:T(8,128)(2,1)S(1)}, bf16[1,384,512]{2,1,0:T(8,128)(2,1)}, u32[]{:S(2)}) copy-start(bf16[1,384,512]{2,1,0:T(8,128)(2,1)} %copy-done.11) | copy-start | bytes 1179652
  63.9 1.8 %copy-start.45 = (f32[1,1,512]{2,0,1:T(1,128)S(1)}, f32[1,1,512]{2,0,1:T(1,128)}, u32[]{:S(2)}) copy-start(f32[1,1,512]{2,0,1:T(1,128)} %get-tuple-element.70) | copy-start | bytes 6148
  63.9 1.8 %copy-start.47 = (f32[1,1,512]{2,0,1:T(1,128)S(1)}, f32[1,1,512]{2,0,1:T(1,128)}, u32[]{:S(2)}) copy-start(f32[1,1,512]{2,0,1:T(1,128)} %get-tuple-element.71) | copy-start | bytes 6148
  64.0 1.8 %copy-start.49 = (f32[1,1,512]{2,0,1:T(1,128)S(1)}, f32[1,1,512]{2,0,1:T(1,128)}, u32[]{:S(2)}) copy-start(f32[1,1,512]{2,0,1:T(1,128)} %get-tuple-element.72) | copy-start | bytes 6148
  65.8 1.6 %copy-start.43 = (f32[2,256]{1,0:T(2,128)S(1)}, f32[2,256]{1,0:T(2,128)}, u32[]{:S(2)}) copy-start(f32[2,256]{1,0:T(2,128)} %slice_bitcast_fusion.5) | copy-start | bytes 6148
  68.6 1.6 %copy-start.2 = (f32[2,512,512]{2,1,0:T(8,128)S(1)}, f32[2,512,512]{2,1,0:T(8,128)}, u32[]{:S(2)}) copy-start(f32[2,512,512]{2,1,0:T(8,128)} %copy-done.1) | copy-start | bytes 6291460
  71.2 1.6 %copy-start.6 = (f32[2,512,512]{2,1,0:T(8,128)S(1)}, f32[2,512,512]{2,1,0:T(8,128)}, u32[]{:S(2)}) copy-start(f32[2,512,512]{2,1,0:T(8,128)} %get-tuple-element.86) | copy-start | bytes 6291460
  71.2 1.6 %copy-start.50 = (bf16[2,256,4]{1,2,0:T(4,128)(2,1)S(1)}, bf16[2,256,4]{1,2,0:T(4,128)(2,1)}, u32[]{:S(2)}) copy-start(bf16[2,256,4]{1,2,0:T(4,128)(2,1)} %slice.294) | copy-start | bytes 12292
  73.6 1.2 %copy-start = (f32[512,512]{1,0:T(8,128)S(1)}, f32[512,512]{1,0:T(8,128)}, u32[]{:S(2)}) copy-start(f32[512,512]{1,0:T(8,128)} %convolution_bitcast_fusion.1.m2) | copy-start | bytes 3145732
  74.8 36.3 %copy-start.21 = (f32[12,512]{1,0:T(8,128)S(1)}, f32[12,512]{1,0:T(8,128)}, u32[]{:S(2)}) copy-start(f32[12,512]{1,0:T(8,128)} %copy-done.20) | copy-start | bytes 73732
  74.8 36.6 %copy-start.42 = (f32[1,512]{1,0:T(1,128)S(1)}, f32[1,512]{1,0:T(1,128)}, u32[]{:S(2)}) copy-start(f32[1,512]{1,0:T(1,128)} %copy-done.41) | copy-start | bytes 6148
  74.8 36.6 %copy-start.57 = (f32[4]{0:T(128)S(1)}, f32[4]{0:T(128)}, u32[]{:S(2)}) copy-start(f32[4]{0:T(128)} %copy-done.56) | copy-start | bytes 52
  74.8 37.0 %copy-start.16 = (bf16[2,512,512]{2,1,0:T(8,128)(2,1)S(1)}, bf16[2,512,512]{2,1,0:T(8,128)(2,1)}, u32[]{:S(2)}) copy-start(bf16[2,512,512]{2,1,0:T(8,128)(2,1)} %param.14) | copy-start | bytes 3145732
  111.0 1.1 copy-start.28
  111.0 1.2 %copy-start.24 = (bf16[2,512,512]{2,1,0:T(8,128)(2,1)S(1)}, bf16[2,512,512]{2,1,0:T(8,128)(2,1)}, u32[]{:S(2)}) copy-start(bf16[2,512,512]{2,1,0:T(8,128)(2,1)} %param.15) | copy-start | bytes 3145732
  (20 other events, 14.9 us)

commit v2 on v0

v2 whole, which is shorter than its diff:
```python
import functools

import jax
import jax.numpy as jnp
from jax import lax
from jax.experimental import pallas as pl
from jax.experimental.pallas import tpu as pltpu
from jax.sharding import PartitionSpec as P

DMAX = 64
EPSILON = 1e-06
F32 = jnp.float32
BF16 = jnp.bfloat16


def turned(a, b):
    return lax.dot_general(a, b, (((0,), (0,)), ((), ())), preferred_element_type=F32)


def dot(a, b):
    return jnp.dot(a, b, preferred_element_type=F32)


def dot_t(a, b):
    return lax.dot_general(a, b, (((1,), (1,)), ((), ())), preferred_element_type=F32)


def parts(a):
    high = a.astype(BF16)
    return high, (a - high.astype(F32)).astype(BF16)


def table_dot(table, w, transposed=False):
    high, low = parts(table)
    both = jnp.concatenate([high, low], axis=0)
    product = dot_t(both, w) if transposed else dot(both, w)
    return product[: table.shape[0]] + product[table.shape[0] :]


class Halving:
    def __init__(self, n, order, me, mats, acc, send, recv, sems):
        self.n, self.order, self.me, self.mats = n, order, me, mats
        self.acc, self.send, self.recv, self.sems = acc, send, recv, sems
        self.left = sorted(order)
        self.base = 0

    def plan(self, j):
        bit_at = self.order[j]
        at = self.left.index(bit_at)
        bit = lax.rem(lax.div(self.me, 1 << bit_at), 2)
        return at, bit, self.me + (1 - 2 * bit) * (1 << bit_at), self.n >> (j + 1)

    def block(self, j, q, at, bit):
        low = 1 << at
        index = lax.div(q, low) * (2 * low) + bit * low + lax.rem(q, low)
        if j > 0:
            return self.acc[index]
        width = self.mats[0].shape[0] // self.n
        rows = pl.ds(pl.multiple_of(index * width, width), width)
        return jnp.concatenate([m[rows, :] for m in self.mats], axis=0)

    def copy(self, j):
        at, bit, partner, count = self.plan(j)
        where = pl.ds(self.base, count)
        return pltpu.make_async_remote_copy(
            src_ref=self.send.at[where],
            dst_ref=self.recv.at[where],
            send_sem=self.sems.at[0, j],
            recv_sem=self.sems.at[1, j],
            device_id={"seq": partner},
            device_id_type=pl.DeviceIdType.MESH,
        )

    def start(self, j):
        at, bit, partner, count = self.plan(j)
        base = self.base

        def pack(q, carry):
            self.send[base + q] = self.block(j, q, at, 1 - bit).astype(self.send.dtype)
            return carry

        lax.fori_loop(0, count, pack, 0)
        self.copy(j).start()

    def finish(self, j):
        at, bit, partner, count = self.plan(j)
        base = self.base
        self.copy(j).wait()

        def fold(q, carry):
            self.acc[q] = self.block(j, q, at, bit) + self.recv[base + q].astype(F32)
            return carry

        lax.fori_loop(0, count, fold, 0)
        self.base += count
        self.left.remove(self.order[j])


def kernel(
    n, steps, dil, codes, emb, gain, taps, up_w, gate_w, out_w, cot,
    out_a, out_b, small_out,
    low_s, second_s, unit_s, inv_s, norm_s, mixed_s, partner_s, hidden_s, gu_s, gl_s, gm_s, gp_s,
    low0_s, hidden0_s, m_out1, m_up1, m_gate1, m_out0,
    acc_a, send_a, recv_a, acc_b, send_b, recv_b, ssend, srecv,
    sems_a, sems_b, sems_s, sems_c,
):
    me = lax.axis_index("seq")
    rows, channels = cot.shape
    half = rows // 2
    full, part = half + 4 * DMAX, half + 2 * DMAX
    mirror = n - 1 - me
    following = lax.rem(me + 1, n)
    previous = lax.rem(me + n - 1, n)
    beyond = lax.rem(n - me, n)
    alone = beyond == me

    barrier = pltpu.get_barrier_semaphore()

    def greet(device):
        pl.semaphore_signal(
            barrier, inc=1, device_id={"seq": device}, device_id_type=pl.DeviceIdType.MESH
        )

    for j in range(steps):
        greet(me + (1 - 2 * lax.rem(lax.div(me, 1 << j), 2)) * (1 << j))
    greet(mirror)
    greet(following)
    greet(previous)

    @pl.when(jnp.logical_not(alone))
    def _():
        greet(beyond)

    pl.semaphore_wait(barrier, steps + 4 - jnp.where(alone, 1, 0))

    def send_rows(src, dst, at, device):
        return pltpu.make_async_remote_copy(
            src_ref=src, dst_ref=dst, send_sem=sems_c.at[0, at], recv_sem=sems_c.at[1, at],
            device_id={"seq": device}, device_id_type=pl.DeviceIdType.MESH,
        )

    near = half + DMAX
    to_mirror = send_rows(cot.at[pl.ds(half - DMAX, near)], second_s.at[pl.ds(0, near)], 0, mirror)
    to_next = send_rows(cot.at[pl.ds(rows - DMAX, DMAX)], low_s.at[pl.ds(0, DMAX)], 1, following)
    to_beyond = send_rows(cot.at[pl.ds(0, DMAX)], second_s.at[pl.ds(near, DMAX)], 2, beyond)
    to_mirror.start()
    to_next.start()

    @pl.when(alone)
    def _():
        own_copy = pltpu.make_async_copy(
            cot.at[pl.ds(0, DMAX)], second_s.at[pl.ds(near, DMAX)], sems_c.at[0, 3]
        )
        own_copy.start()
        own_copy.wait()

    @pl.when(jnp.logical_not(alone))
    def _():
        to_beyond.start()

    low_s[DMAX:part, :] = cot[0:near, :]

    embedded = emb[...]
    wide0 = embedded.astype(F32)
    unit0 = wide0 * lax.rsqrt(jnp.mean(wide0 * wide0, axis=-1, keepdims=True) + EPSILON)
    table = (unit0 * gain[0:1, :]).astype(BF16)
    table_wide = table.astype(F32)
    tapped = jnp.concatenate([taps[0, k : k + 1, :] * table_wide for k in range(3)], axis=0)
    tapped = jnp.concatenate([tapped, jnp.zeros((4, channels), F32)], axis=0)
    up_high, up_low = parts(table_dot(tapped, up_w[0]))
    gates = jax.nn.sigmoid(dot(jnp.concatenate([table_wide] * 4, axis=0).astype(BF16), gate_w[0]))
    row_of = lax.broadcasted_iota(jnp.int32, (16, channels), 0)
    gate_high, gate_low = parts(jnp.where(row_of >= 12, gates, 0.0))
    up_table = jnp.concatenate([up_high, up_low], axis=0)
    gate_table = jnp.concatenate([gate_high, gate_low], axis=0)
    embed_table = jnp.where(
        (row_of >= 4) & (row_of < 8), jnp.concatenate([wide0] * 4, axis=0), 0.0
    ).astype(BF16)
    hot_rows = lax.broadcasted_iota(jnp.int32, (16, 128), 0)

    def hot_at(start):
        code = codes[:, pl.ds(pl.multiple_of(start, 128), 128)]
        return jnp.where(code == lax.rem(hot_rows, 4), 1.0, 0.0)

    def block0(hot):
        two = jnp.concatenate([hot, hot], axis=0).astype(BF16)
        return turned(two, up_table), turned(two, gate_table)

    first_row = lax.broadcasted_iota(jnp.int32, (128, 1), 0)

    def forward0(c, carry):
        start = pl.multiple_of(c * 128, 128)
        hot = hot_at(start)
        upward0, gate0 = block0(hot)
        hidden0 = (upward0 * gate0).astype(BF16)
        wide = turned(hot.astype(BF16), embed_table) + dot(hidden0, out_w[0])
        wide = wide.astype(BF16).astype(F32)
        inverse = lax.rsqrt(jnp.mean(wide * wide, axis=-1, keepdims=True) + EPSILON)
        unit = wide * inverse
        place = me * rows - 2 * DMAX + lax.rem(start, full) + first_row
        normed = jnp.where(place >= 0, unit * gain[1:2, :], 0.0).astype(BF16)
        at = pl.ds(start, 128)
        unit_s[at, :] = unit
        inv_s[at, :] = jnp.broadcast_to(inverse, (128, 128))
        norm_s[at, :] = normed
        return carry

    lax.fori_loop(0, 2 * full // 128, forward0, 0)

    to_mirror.wait()
    to_next.wait()

    @pl.when(jnp.logical_not(alone))
    def _():
        to_beyond.wait()

    up = lax.broadcasted_iota(jnp.int32, (part, part), 0)
    down = lax.broadcasted_iota(jnp.int32, (part, part), 1)
    flip = jnp.where(up + down == part - 1, 1.0, 0.0).astype(BF16)
    edge_row = lax.broadcasted_iota(jnp.int32, (DMAX, 1), 0)
    within = me * rows - DMAX + edge_row >= 0
    low_s[part : 2 * part, :] = dot(flip, second_s[...]).astype(BF16)
    for p in range(2):
        edge = low_s[p * part : p * part + DMAX, :].astype(F32)
        low_s[p * part : p * part + DMAX, :] = jnp.where(within, edge, 0.0).astype(BF16)

    d1 = dil[1]
    tap = [taps[1, k : k + 1, :] for k in range(3)]

    to_row = lax.broadcasted_iota(jnp.int32, (128, 256), 0)
    from_row = lax.broadcasted_iota(jnp.int32, (128, 256), 1)
    distance = from_row - to_row - DMAX

    def shifted(ref, at, offset):
        window = ref[pl.ds(pl.multiple_of(at - DMAX, 64), 256), :]
        move = jnp.where(distance == offset, 1.0, 0.0).astype(BF16)
        return dot(move, window)

    def middle(c, carry):
        p = lax.div(c, part // 128)
        r0 = lax.rem(c, part // 128) * 128
        sign = 1 - 2 * p
        begin = p * full + DMAX + r0
        mixed = tap[0] * shifted(norm_s, begin, -sign * d1)
        mixed = mixed + tap[1] * norm_s[pl.ds(pl.multiple_of(begin, 64), 128), :].astype(F32)
        mixed = (mixed + tap[2] * shifted(norm_s, begin, sign * d1)).astype(BF16)
        other = pl.multiple_of((1 - p) * full + DMAX + r0, 64)
        partner = norm_s[pl.ds(other, 128), :]
        at = pl.ds(pl.multiple_of(c * 128, 128), 128)
        upward = dot(mixed, up_w[1])
        gate = jax.nn.sigmoid(dot(partner, gate_w[1]))
        grad_hidden = dot_t(low_s[at, :], out_w[1])
        gated = grad_hidden * gate
        gu = gated.astype(BF16)
        gl = (gated * upward * (1.0 - gate)).astype(BF16)
        mixed_s[at, :] = mixed
        partner_s[at, :] = partner
        hidden_s[at, :] = (upward * gate).astype(BF16)
        gu_s[at, :] = gu
        gl_s[at, :] = gl
        gm_s[at, :] = dot_t(gu, up_w[1]).astype(BF16)
        gp_s[at, :] = dot_t(gl, gate_w[1]).astype(BF16)
        return carry

    lax.fori_loop(0, 2 * part // 128, middle, 0)

    def own(ref, cols=slice(None)):
        return jnp.concatenate(
            [ref[DMAX : DMAX + half, cols], ref[part + DMAX : part + DMAX + half, cols]], axis=0
        )

    def rows_into(mat, left, right, pick):
        whole = pick(right)
        for c in range(channels // 256):
            cols = slice(c * 256, c * 256 + 256)
            mat[cols, :] = turned(pick(left, cols), whole)

    rows_into(m_out1, low_s, hidden_s, own)
    rows_into(m_up1, gu_s, mixed_s, own)
    rows_into(m_gate1, gl_s, partner_s, own)

    order_a = list(range(steps))
    order_b = [0] + order_a[2:] + [1]
    first = Halving(n, order_a, me, (m_out1, m_up1, m_gate1), acc_a, send_a, recv_a, sems_a)
    first.start(0)

    small_out[...] = jnp.zeros_like(small_out)

    def backward(c, carry):
        p = lax.div(c, half // 128)
        r0 = lax.rem(c, half // 128) * 128
        sign = 1 - 2 * p
        mine = p * part + DMAX + r0
        mine_at = pl.ds(pl.multiple_of(mine, 64), 128)
        here = p * full + 2 * DMAX + r0
        here_at = pl.ds(pl.multiple_of(here, 64), 128)
        grad_mixed = gm_s[mine_at, :].astype(F32)
        grad_normed = tap[0] * shifted(gm_s, mine, sign * d1)
        grad_normed = grad_normed + tap[1] * grad_mixed
        grad_normed = grad_normed + tap[2] * shifted(gm_s, mine, -sign * d1)
        other = pl.multiple_of((1 - p) * part + DMAX + r0, 64)
        grad_normed = grad_normed + gp_s[pl.ds(other, 128), :].astype(F32)
        unit = unit_s[here_at, :]
        sums = [
            jnp.sum(grad_mixed * shifted(norm_s, here, -sign * d1), axis=0, keepdims=True),
            jnp.sum(grad_mixed * norm_s[here_at, :].astype(F32), axis=0, keepdims=True),
            jnp.sum(grad_mixed * shifted(norm_s, here, sign * d1), axis=0, keepdims=True),
            jnp.sum(grad_normed * unit, axis=0, keepdims=True),
            jnp.zeros((4, channels), F32),
        ]
        grad_unit = grad_normed * gain[1:2, :]
        average = jnp.mean(grad_unit * unit, axis=-1, keepdims=True)
        gradient = low_s[mine_at, :].astype(F32) + inv_s[here_at, 0:1] * (
            grad_unit - unit * average
        )
        low0, rest0 = parts(gradient)
        grad_hidden0 = dot_t(low0, out_w[0])
        hot = hot_at(here)
        upward0, gate0 = block0(hot)
        gated = grad_hidden0 * gate0
        gu0 = gated.astype(BF16)
        gl0 = (gated * upward0 * (1.0 - gate0)).astype(BF16)
        hot_up = jnp.where(hot_rows < 12, hot, 0.0).astype(BF16)
        hot_gate = jnp.where(hot_rows < 12, 0.0, hot).astype(BF16)
        hot16 = hot.astype(BF16)
        small_out[0:16, :] += dot(hot_up, gu0) + dot(hot_gate, gl0)
        small_out[16:24, :] += (dot(hot16, low0) + dot(hot16, rest0))[0:8]
        small_out[24:32, :] += jnp.concatenate(sums, axis=0)
        at = pl.ds(pl.multiple_of(c * 128, 128), 128)
        low0_s[at, :] = low0
        hidden0_s[at, :] = (upward0 * gate0).astype(BF16)
        return carry

    lax.fori_loop(0, 2 * half // 128, backward, 0)

    first.finish(0)
    first.start(1)
    rows_into(m_out0, low0_s, hidden0_s, lambda ref, cols=slice(None): ref[:, cols])
    second = Halving(n, order_b, me, (m_out0,), acc_b, send_b, recv_b, sems_b)

    def small_copy(j):
        partner = second.plan(j)[2]
        return pltpu.make_async_remote_copy(
            src_ref=ssend.at[j], dst_ref=srecv.at[j],
            send_sem=sems_s.at[0, j], recv_sem=sems_s.at[1, j],
            device_id={"seq": partner}, device_id_type=pl.DeviceIdType.MESH,
        )

    for j in range(steps):
        ssend[j] = small_out[...]
        small_copy(j).start()
        second.start(j)
        if j + 1 < steps:
            if j > 0:
                first.start(j + 1)
            first.finish(j + 1) if j == 0 else None
        small_copy(j).wait()
        small_out[...] = small_out[...] + srecv[j]
        second.finish(j)
        if 0 < j and j + 1 < steps:
            first.finish(j + 1)
    out_a[...] = acc_a[0]
    out_b[...] = acc_b[0]


def fused(dilations, codes, embedding, norm_gain, conv_taps, w_up, w_gate, w_out, cotangent):
    n = lax.axis_size("seq")
    steps = n.bit_length() - 1
    rows, channels = cotangent.shape
    half = rows // 2
    full, part = 2 * (half + 4 * DMAX), 2 * (half + 2 * DMAX)
    width = channels // n
    vmem = pl.BlockSpec(memory_space=pltpu.VMEM)

    def wide(count, kind=F32, cols=channels):
        return pltpu.VMEM((count, cols), kind)

    def buffers(mats):
        return [
            pltpu.VMEM((n // 2, mats * width, channels), F32),
            pltpu.VMEM((n - 1, mats * width, channels), BF16 if mats * width % 16 == 0 else F32),
            pltpu.VMEM((n - 1, mats * width, channels), BF16 if mats * width % 16 == 0 else F32),
        ]

    sems = pltpu.SemaphoreType.DMA
    return pl.pallas_call(
        functools.partial(kernel, n, steps),
        out_shape=(
            jax.ShapeDtypeStruct((3 * width, channels), F32),
            jax.ShapeDtypeStruct((width, channels), F32),
            jax.ShapeDtypeStruct((32, channels), F32),
        ),
        in_specs=[pl.BlockSpec(memory_space=pltpu.SMEM)] + [vmem] * 8,
        out_specs=(vmem,) * 3,
        scratch_shapes=[
            wide(part, BF16), wide(part // 2, BF16),
            wide(full), wide(full, F32, 128), wide(full, BF16),
            *[wide(part, BF16) for _ in range(5)],
            wide(part, BF16), wide(part, BF16),
            wide(2 * half, BF16), wide(2 * half, BF16),
            *[wide(channels) for _ in range(4)],
            *buffers(3), *buffers(1),
            pltpu.VMEM((steps, 32, channels), F32), pltpu.VMEM((steps, 32, channels), F32),
            sems((2, steps)), sems((2, steps)), sems((2, steps)), sems((2, 4)),
        ],
        compiler_params=pltpu.CompilerParams(
            collective_id=0, has_side_effects=True, vmem_limit_bytes=56 * 1024 * 1024
        ),
    )(dilations, codes, embedding, norm_gain, conv_taps, w_up, w_gate, w_out, cotangent)


def per_device(tokens, dilations, embedding, norm_gain, conv_taps, w_up, w_gate, w_out, cotangent):
    n = lax.axis_size("seq")
    me = lax.axis_index("seq")
    rows = tokens.shape[0]
    half = rows // 2
    channels = embedding.shape[1]
    to_mirror = [(i, n - 1 - i) for i in range(n)]
    to_next = [(i, (i + 1) % n) for i in range(n)]
    to_beyond = [(i, (n - i) % n) for i in range(n)]

    tok_prev = lax.ppermute(tokens, "seq", to_next)
    tok_mirror = lax.ppermute(tokens, "seq", to_mirror)
    tok_beyond = lax.ppermute(tokens, "seq", to_beyond)
    edge = 3 * DMAX
    tok = jnp.stack(
        [
            jnp.concatenate([tok_prev[rows - edge :], tokens[: half + edge]]),
            jnp.flip(jnp.concatenate([tok_mirror[half - edge :], tok_beyond[:edge]])),
        ]
    )
    position = me * rows - edge + jnp.arange(half + 2 * edge, dtype=jnp.int32)
    inside = position >= 0
    tok = jnp.where(inside[None], tok, -1)
    d0 = dilations[0]
    count1 = half + 4 * DMAX
    codes = []
    for k in range(3):
        shift = (k - 1) * d0
        codes.append(
            jnp.concatenate(
                [
                    lax.dynamic_slice_in_dim(tok[0], DMAX + shift, count1, 0),
                    lax.dynamic_slice_in_dim(tok[1], DMAX - shift, count1, 0),
                ]
            )
        )
    codes.append(tok[::-1, DMAX : DMAX + count1].reshape(-1))
    codes = jnp.repeat(jnp.stack(codes), 4, axis=0)
    mats, mat_b, small = fused(
        dilations, codes, embedding, norm_gain, conv_taps, w_up, w_gate, w_out, cotangent
    )

    wide0 = embedding.astype(F32)
    inverse0 = lax.rsqrt(jnp.mean(wide0 * wide0, axis=-1, keepdims=True) + EPSILON)
    unit0 = wide0 * inverse0
    table_wide = (unit0 * norm_gain[0]).astype(BF16).astype(F32)
    tapped = (conv_taps[0][:, None, :] * table_wide[None]).reshape(12, channels)

    width = channels // n
    sum_up, sum_logit, sum_grad = small[:12], small[12:16], small[20:24]
    columns = jnp.concatenate([sum_up, sum_logit], axis=0)
    mine = lax.dynamic_slice_in_dim(columns, me * width, width, 1)
    exact = functools.partial(
        lax.dot_general,
        dimension_numbers=(((0,), (0,)), ((), ())),
        precision=lax.Precision.HIGHEST,
        preferred_element_type=F32,
    )
    out0 = mat_b.T
    out1, up1, gate1 = [m.T for m in mats.reshape(3, width, channels)]
    grad_up = jnp.stack([exact(tapped, mine[:12]), up1])
    grad_gate = jnp.stack([exact(table_wide, mine[12:]), gate1])
    grad_out = jnp.stack([out0, out1])

    spread = table_dot(sum_up, w_up[0], True).reshape(3, 4, channels)
    grad_normed0 = jnp.sum(conv_taps[0][:, None, :] * spread, axis=0)
    grad_normed0 = grad_normed0 + table_dot(sum_logit, w_gate[0], True)
    grad_taps = jnp.stack([jnp.sum(spread * table_wide[None], axis=1), small[24:27]])
    grad_gain = jnp.stack([jnp.sum(grad_normed0 * unit0, axis=0), small[27]])
    grad_unit0 = grad_normed0 * norm_gain[0]
    grad_embed = sum_grad + inverse0 * (
        grad_unit0 - unit0 * jnp.mean(grad_unit0 * unit0, axis=-1, keepdims=True)
    )
    return (grad_up, grad_gate, grad_out, grad_taps, grad_gain, grad_embed)


def solution(mesh):
    in_specs = (P(("groups", "seq")), P(), P(), P(), P(), P(), P(), P(), P(("groups", "seq"), None))
    out_specs = (
        P("groups", None, "seq"),
        P("groups", None, "seq"),
        P("groups", None, "seq"),
        P("groups", None, None),
        P("groups", None),
        P("groups", None),
    )
    return jax.shard_map(
        per_device, mesh=mesh, in_specs=in_specs, out_specs=out_specs, check_vma=False
    )
```

time: 366 us -> 101 us (0.28)
  the two profiles are of different devices: /device:TPU:0 before, /device:TPU:24 now
where the time goes in v2:
time: 101 us; the launch traced here: 99.7 us
  Pallas kernels  72.2 us (71%)
  local copies, waits for them, and re-layouts  11.4 us (11%)
  starting transfers between devices  7.69 us (8%)
  other arithmetic  6.31 us (6%)
  matrix products  1.1 us (1%)
  between operations  1.04 us (1%)
    pallas_call x1, Pallas kernels, fused(): pl.pallas_call(functools.partial(kernel, n, steps), out_shape=(jax.ShapeD...  72.2 us
    unnamed x24, local copies, waits for them, and re-layouts  5.54 us
    ppermute x1, starting transfers between devices, per_device(): tok_mirror = lax.ppermute(tokens, 'seq', to_mirror)  5.38 us
    ppermute x1, starting transfers between devices, per_device(): tok_beyond = lax.ppermute(tokens, 'seq', to_beyond)  2.25 us
  transfers between devices with their start and end apart: 3, of which 0 were waited for; matrix products, arithmetic and copies ran while one was open for 1% of the time, Pallas kernels for 0%

profile of v2, /device:TPU:24, one launch (start us, length us, event | category | flops | bytes accessed | tf_op | source)
XLA Modules:
  0.0 99.7 jit_solution(180268261826889046)
XLA Ops:
  0.6 0.0 copy-start.2
  0.6 0.1 collective-permute-start
  0.7 2.2 %collective-permute-start.2 = (s32[512]{0:T(512)}, s32[512]{0:T(512)S(1)}, u32[]{:S(2)}, u32[]{:S(2)}) collective-permute-start(s32[512]{0:T(512)} %param.9), channel_id=1, source_target_pairs={{0,0},{1,15},{2,14},{3,13},{4,12},{5,11},{6,10},{7,9},{8,8},{9,7},... | collective-permute-start | bytes 6152 | tf_op jit(solution)/shard_map/ppermute | solution.py:424
  3.0 5.4 %collective-permute-start.1 = (s32[512]{0:T(512)}, s32[512]{0:T(512)S(1)}, u32[]{:S(2)}, u32[]{:S(2)}) collective-permute-start(s32[512]{0:T(512)} %param.9), channel_id=1, source_target_pairs={{0,15},{1,14},{2,13},{3,12},{4,11},{5,10},{6,9},{7,8},{8,7},{9,6},... | collective-permute-start | bytes 6152 | tf_op jit(solution)/shard_map/ppermute | solution.py:423
  8.4 0.1 fusion.19
  8.5 0.7 copy-done.6
  9.2 0.1 fusion.30
  9.2 0.7 copy-done.9
  10.0 0.0 copy-start.5
  10.1 0.6 copy-done.5
  10.7 0.6 copy.17.taps
  11.3 0.7 slice-done
  12.0 0.0 collective-permute-done
  12.0 0.1 slice.85
  12.1 0.6 copy-done.8
  12.7 0.1 pad_add_fusion.1
  12.8 0.6 copy-done.7
  13.4 0.1 slice.87
  13.4 0.6 slice-done.1
  14.0 0.1 pad_add_fusion.2
  14.1 0.1 rev.7
  14.2 0.1 slice.108
  14.3 0.1 fusion.32
  14.4 0.1 rev.8
  14.6 0.1 constant_dynamic-slice_fusion.2
  14.7 0.7 reshape.72.codes
  15.4 72.2 %shard_map.136 = (f32[96,512]{1,0:T(8,128)}, f32[32,512]{1,0:T(8,128)}, f32[32,512]{1,0:T(8,128)}) custom-call(s32[2]{0:T(128)} %dil.1, s32[16,1024]{1,0:T(8,128)} %reshape.72.codes, bf16[4,512]{1,0:T(4,128)(2,1)} %emb.1, f32[2,512]{1,0:T(2,128)} %gain.1, f32[2,3,512]{2,1,0:T(4,128)} %copy.17.taps, bf16[2,512,512]{2,1,0:T(8,128)(2,1)} %up_w.1, ...), custom_call_target="tpu_custom_call" | custom-call | tf_op jit(solution)/shard_map/pallas_call | solution.py:386
  87.6 0.0 copy-start.1
  87.6 0.8 slice.104
  88.4 0.7 slice_bitcast_fusion.3
  89.1 0.8 subtract_convert_fusion.1
  89.9 0.8 concatenate.29
  90.7 0.8 subtract_convert_fusion
  91.5 0.9 slice_bitcast_fusion
  92.5 0.2 fusion.2
  92.8 0.2 fusion
  93.0 0.1 multiply_reduce_fusion
  93.1 0.7 copy-done.3
  93.7 0.2 fusion.15
  93.9 0.6 copy.18
  94.5 0.3 convolution_bitcast_fusion.1
  94.9 0.3 convolution_bitcast_fusion
  95.2 0.5 copy-done.4
  95.7 0.7 pad_maximum_fusion.2
  96.4 1.4 %fusion.18 = f32[4,512]{1,0:T(4,128)} fusion(bf16[4,512]{1,0:T(4,128)(2,1)S(1)} %copy-done.3, f32[32,512]{1,0:T(8,128)} %get-tuple-element.9, f32[4,512]{1,0:T(4,128)S(1)} %get-tuple-element.28, f32[4]{0:T(128)S(1)} %broadcast_multiply_fusion.1, f32[512]{0:T(512)S(1)} %bitcast.62, f32[4]{0:T(128)S(1)} %add_rsqrt_fusion), kind=kLoop, calls=%fused_computation.36 | loop fusion | flops 14336 | bytes 30752 | tf_op jit(solution)/shard_map/add | solution.py:482
  97.8 0.6 pad_maximum_fusion.4
  98.4 0.7 pad_maximum_fusion
  99.0 0.7 pad_maximum_fusion.1
  (33 shorter events, 0.2 us)
Async XLA Ops:
  0.6 7.7 %copy-start.2 = (bf16[4,512]{1,0:T(4,128)(2,1)S(1)}, bf16[4,512]{1,0:T(4,128)(2,1)}, u32[]{:S(2)}) copy-start(bf16[4,512]{1,0:T(4,128)(2,1)} %emb.1) | copy-start | bytes 12292
  0.6 11.4 %collective-permute-start = (s32[512]{0:T(512)}, s32[512]{0:T(512)S(1)}, u32[]{:S(2)}, u32[]{:S(2)}) collective-permute-start(s32[512]{0:T(512)} %param.9), channel_id=1, source_target_pairs={{0,1},{1,2},{2,3},{3,4},{4,5},{5,6},{6,7},{7,8},{8,9},{9,10},{10,1... | collective-permute-start | bytes 6152 | tf_op jit(solution)/shard_map/ppermute | solution.py:422
  0.7 12.1 %collective-permute-start.2 = (s32[512]{0:T(512)}, s32[512]{0:T(512)S(1)}, u32[]{:S(2)}, u32[]{:S(2)}) collective-permute-start(s32[512]{0:T(512)} %param.9), channel_id=1, source_target_pairs={{0,0},{1,15},{2,14},{3,13},{4,12},{5,11},{6,10},{7,9},{8,8},{9,7},... | collective-permute-start | bytes 6152 | tf_op jit(solution)/shard_map/ppermute | solution.py:424
  3.0 10.4 %collective-permute-start.1 = (s32[512]{0:T(512)}, s32[512]{0:T(512)S(1)}, u32[]{:S(2)}, u32[]{:S(2)}) collective-permute-start(s32[512]{0:T(512)} %param.9), channel_id=1, source_target_pairs={{0,15},{1,14},{2,13},{3,12},{4,11},{5,10},{6,9},{7,8},{8,7},{9,6},... | collective-permute-start | bytes 6152 | tf_op jit(solution)/shard_map/ppermute | solution.py:423
  8.5 0.7 copy-start.6
  9.2 0.7 copy-start.9
  10.0 0.7 copy-start.5
  11.3 0.7 slice-start
  12.0 0.7 copy-start.8
  12.8 0.6 copy-start.7
  13.4 0.7 slice-start.1
  15.4 77.1 %copy-start = (bf16[2,512,512]{2,1,0:T(8,128)(2,1)S(1)}, bf16[2,512,512]{2,1,0:T(8,128)(2,1)}, u32[]{:S(2)}) copy-start(bf16[2,512,512]{2,1,0:T(8,128)(2,1)} %up_w.1) | copy-start | bytes 3145732
  87.6 5.2 %copy-start.1 = (bf16[2,512,512]{2,1,0:T(8,128)(2,1)S(1)}, bf16[2,512,512]{2,1,0:T(8,128)(2,1)}, u32[]{:S(2)}) copy-start(bf16[2,512,512]{2,1,0:T(8,128)(2,1)} %gate_w.1) | copy-start | bytes 3145732
  93.0 0.7 copy-start.3
  94.9 0.8 copy-start.4

commit v3 on v2

--- a/solution.py
+++ b/solution.py
@@ -98,7 +98,8 @@
 
 def kernel(
     n, steps, dil, codes, emb, gain, taps, up_w, gate_w, out_w, cot,
-    out_a, out_b, small_out,
+    out_a, out_b, out_c, out_taps, out_gain, out_embed,
+    small_out,
     low_s, second_s, unit_s, inv_s, norm_s, mixed_s, partner_s, hidden_s, gu_s, gl_s, gm_s, gp_s,
     low0_s, hidden0_s, m_out1, m_up1, m_gate1, m_out0,
     acc_a, send_a, recv_a, acc_b, send_b, recv_b, ssend, srecv,
@@ -162,7 +163,8 @@
 
     embedded = emb[...]
     wide0 = embedded.astype(F32)
-    unit0 = wide0 * lax.rsqrt(jnp.mean(wide0 * wide0, axis=-1, keepdims=True) + EPSILON)
+    inverse0 = lax.rsqrt(jnp.mean(wide0 * wide0, axis=-1, keepdims=True) + EPSILON)
+    unit0 = wide0 * inverse0
     table = (unit0 * gain[0:1, :]).astype(BF16)
     table_wide = table.astype(F32)
     tapped = jnp.concatenate([taps[0, k : k + 1, :] * table_wide for k in range(3)], axis=0)
@@ -362,6 +364,38 @@
     out_a[...] = acc_a[0]
     out_b[...] = acc_b[0]
 
+    sums = small_out[0:16, :]
+    width = channels // n
+    pick = jnp.where(
+        lax.broadcasted_iota(jnp.int32, (width, channels), 1)
+        == me * width + lax.broadcasted_iota(jnp.int32, (width, channels), 0),
+        1.0,
+        0.0,
+    )
+
+    def exact(a, b, dims):
+        return lax.dot_general(
+            a, b, (dims, ((), ())), precision=lax.Precision.HIGHEST, preferred_element_type=F32
+        )
+
+    mine = exact(pick, sums, ((1,), (1,)))
+    gate_rows = jnp.where(row_of >= 12, jnp.concatenate([table_wide] * 4, axis=0), 0.0)
+    out_c[0:width, :] = exact(mine, tapped, ((1,), (0,)))
+    out_c[width : 2 * width, :] = exact(mine, gate_rows, ((1,), (0,)))
+    spread = table_dot(sums, up_w[0], True)
+    grad_normed0 = table_dot(sums, gate_w[0], True)[12:16]
+    for k in range(3):
+        own_rows = spread[4 * k : 4 * k + 4]
+        grad_normed0 = grad_normed0 + taps[0, k : k + 1, :] * own_rows
+        out_taps[0, k : k + 1, :] = jnp.sum(own_rows * table_wide, axis=0, keepdims=True)
+    out_taps[1] = small_out[24:27, :]
+    out_gain[0:1, :] = jnp.sum(grad_normed0 * unit0, axis=0, keepdims=True)
+    out_gain[1:2, :] = small_out[27:28, :]
+    grad_unit0 = grad_normed0 * gain[0:1, :]
+    out_embed[...] = small_out[20:24, :] + inverse0 * (
+        grad_unit0 - unit0 * jnp.mean(grad_unit0 * unit0, axis=-1, keepdims=True)
+    )
+
 
 def fused(dilations, codes, embedding, norm_gain, conv_taps, w_up, w_gate, w_out, cotangent):
     n = lax.axis_size("seq")
@@ -388,12 +422,15 @@
         out_shape=(
             jax.ShapeDtypeStruct((3 * width, channels), F32),
             jax.ShapeDtypeStruct((width, channels), F32),
-            jax.ShapeDtypeStruct((32, channels), F32),
+            jax.ShapeDtypeStruct((2 * width, channels), F32),
+            jax.ShapeDtypeStruct(conv_taps.shape, F32),
+            jax.ShapeDtypeStruct(norm_gain.shape, F32),
+            jax.ShapeDtypeStruct(embedding.shape, F32),
         ),
         in_specs=[pl.BlockSpec(memory_space=pltpu.SMEM)] + [vmem] * 8,
-        out_specs=(vmem,) * 3,
+        out_specs=(vmem,) * 6,
         scratch_shapes=[
-            wide(part, BF16), wide(part // 2, BF16),
+            wide(32), wide(part, BF16), wide(part // 2, BF16),
             wide(full), wide(full, F32, 128), wide(full, BF16),
             *[wide(part, BF16) for _ in range(5)],
             wide(part, BF16), wide(part, BF16),
@@ -447,41 +484,15 @@
         )
     codes.append(tok[::-1, DMAX : DMAX + count1].reshape(-1))
     codes = jnp.repeat(jnp.stack(codes), 4, axis=0)
-    mats, mat_b, small = fused(
+    mats, mat_b, mat_c, grad_taps, grad_gain, grad_embed = fused(
         dilations, codes, embedding, norm_gain, conv_taps, w_up, w_gate, w_out, cotangent
     )
-
-    wide0 = embedding.astype(F32)
-    inverse0 = lax.rsqrt(jnp.mean(wide0 * wide0, axis=-1, keepdims=True) + EPSILON)
-    unit0 = wide0 * inverse0
-    table_wide = (unit0 * norm_gain[0]).astype(BF16).astype(F32)
-    tapped = (conv_taps[0][:, None, :] * table_wide[None]).reshape(12, channels)
-
     width = channels // n
-    sum_up, sum_logit, sum_grad = small[:12], small[12:16], small[20:24]
-    columns = jnp.concatenate([sum_up, sum_logit], axis=0)
-    mine = lax.dynamic_slice_in_dim(columns, me * width, width, 1)
-    exact = functools.partial(
-        lax.dot_general,
-        dimension_numbers=(((0,), (0,)), ((), ())),
-        precision=lax.Precision.HIGHEST,
-        preferred_element_type=F32,
-    )
-    out0 = mat_b.T
-    out1, up1, gate1 = [m.T for m in mats.reshape(3, width, channels)]
-    grad_up = jnp.stack([exact(tapped, mine[:12]), up1])
-    grad_gate = jnp.stack([exact(table_wide, mine[12:]), gate1])
-    grad_out = jnp.stack([out0, out1])
-
-    spread = table_dot(sum_up, w_up[0], True).reshape(3, 4, channels)
-    grad_normed0 = jnp.sum(conv_taps[0][:, None, :] * spread, axis=0)
-    grad_normed0 = grad_normed0 + table_dot(sum_logit, w_gate[0], True)
-    grad_taps = jnp.stack([jnp.sum(spread * table_wide[None], axis=1), small[24:27]])
-    grad_gain = jnp.stack([jnp.sum(grad_normed0 * unit0, axis=0), small[27]])
-    grad_unit0 = grad_normed0 * norm_gain[0]
-    grad_embed = sum_grad + inverse0 * (
-        grad_unit0 - unit0 * jnp.mean(grad_unit0 * unit0, axis=-1, keepdims=True)
-    )
+    out1, up1, gate1 = mats.reshape(3, width, channels)
+    up0, gate0 = mat_c.reshape(2, width, channels)
+    grad_up = jnp.stack([up0, up1]).transpose(0, 2, 1)
+    grad_gate = jnp.stack([gate0, gate1]).transpose(0, 2, 1)
+    grad_out = jnp.stack([mat_b, out1]).transpose(0, 2, 1)
     return (grad_up, grad_gate, grad_out, grad_taps, grad_gain, grad_embed)
 
 

time: 101 us -> 93.6 us (0.927)
  the two profiles are of different devices: /device:TPU:24 before, /device:TPU:0 now
where the time goes in v3:
time: 93.6 us; the launch traced here: 93.2 us
  Pallas kernels  72.2 us (77%)
  starting transfers between devices  9.15 us (10%)
  local copies, waits for them, and re-layouts  8.68 us (9%)
  other arithmetic  2.21 us (2%)
  between operations  0.95 us (1%)
    pallas_call x1, Pallas kernels, fused(): pl.pallas_call(functools.partial(kernel, n, steps), out_shape=(jax.ShapeD...  72.2 us
    ppermute x1, starting transfers between devices, per_device(): tok_mirror = lax.ppermute(tokens, 'seq', to_mirror)  7.32 us
    unnamed x23, local copies, waits for them, and re-layouts  5.85 us
  transfers between devices with their start and end apart: 3, of which 0 were waited for; matrix products, arithmetic and copies ran while one was open for 1% of the time, Pallas kernels for 0%

profile of v3, /device:TPU:0, one launch (start us, length us, event | category | flops | bytes accessed | tf_op | source)
XLA Modules:
  0.0 93.2 jit_solution(17732308713895886585)
XLA Ops:
  0.6 0.5 collective-permute-start
  1.1 1.3 %collective-permute-start.2 = (s32[512]{0:T(512)}, s32[512]{0:T(512)S(1)}, u32[]{:S(2)}, u32[]{:S(2)}) collective-permute-start(s32[512]{0:T(512)} %param.9), channel_id=1, source_target_pairs={{0,0},{1,15},{2,14},{3,13},{4,12},{5,11},{6,10},{7,9},{8,8},{9,7},... | collective-permute-start | bytes 6152 | tf_op jit(solution)/shard_map/ppermute | solution.py:461
  2.5 7.3 %collective-permute-start.1 = (s32[512]{0:T(512)}, s32[512]{0:T(512)S(1)}, u32[]{:S(2)}, u32[]{:S(2)}) collective-permute-start(s32[512]{0:T(512)} %param.9), channel_id=1, source_target_pairs={{0,15},{1,14},{2,13},{3,12},{4,11},{5,10},{6,9},{7,8},{8,7},{9,6},... | collective-permute-start | bytes 6152 | tf_op jit(solution)/shard_map/ppermute | solution.py:460
  9.8 0.0 copy-start.8
  9.8 0.7 copy-done.8
  10.6 0.0 copy-start.3
  10.7 0.6 copy-done.3
  11.3 0.6 copy.15.taps
  11.9 0.0 copy-start.7
  11.9 0.0 collective-permute-done
  11.9 0.1 slice.37
  12.0 0.6 copy-done.7
  12.6 0.1 pad_add_fusion.1
  12.7 0.0 collective-permute-done.2
  12.7 0.0 copy-start.5
  12.7 0.6 copy-done.5
  13.3 0.0 collective-permute-done.1
  13.3 0.0 slice-start
  13.3 0.1 slice.39
  13.3 0.6 slice-done
  13.9 0.1 pad_add_fusion.2
  14.0 0.1 rev.7
  14.1 0.1 slice.47
  14.2 0.1 fusion
  14.3 0.1 rev.8
  14.5 0.1 constant_dynamic-slice_fusion.2
  14.6 0.7 reshape.51.codes
  15.3 72.2 %shard_map.136 = (f32[96,512]{1,0:T(8,128)}, f32[32,512]{1,0:T(8,128)}, f32[64,512]{1,0:T(8,128)}, f32[2,3,512]{2,1,0:T(4,128)}, f32[2,512]{1,0:T(2,128)}, /*index=5*/f32[4,512]{1,0:T(4,128)}) custom-call(s32[2]{0:T(128)} %dil.1, s32[16,1024]{1,0:T(8,128)} %reshape.51.codes, bf16[4,512]{1,0:T(4,128)(2,1)} %emb.1, f32[2,512]{1,0:T(2,128)} %gain.1, ...), custom_call_target="tpu_custom_call" | custom-call | tf_op jit(solution)/shard_map/pallas_call | solution.py:420
  87.5 0.0 copy-start
  87.5 0.0 copy-start.2
  87.5 0.9 slice_bitcast_fusion.2
  88.5 0.0 copy-done.2
  88.5 0.6 copy.16
  89.1 0.0 copy-done
  89.1 0.0 copy-start.1
  89.1 0.8 copy-done.1
  89.9 0.7 maximum_bitcast_fusion.2
  90.6 0.7 maximum_bitcast_fusion.1
  91.2 0.0 copy-start.6
  91.2 0.7 maximum_bitcast_fusion
  91.9 0.0 copy-done.6
  91.9 0.0 copy-start.4
  91.9 0.6 copy.20
  92.5 0.1 copy-done.4
  92.6 0.6 copy.21
  (12 shorter events, 0.1 us)
Async XLA Ops:
  0.6 11.3 %collective-permute-start = (s32[512]{0:T(512)}, s32[512]{0:T(512)S(1)}, u32[]{:S(2)}, u32[]{:S(2)}) collective-permute-start(s32[512]{0:T(512)} %param.9), channel_id=1, source_target_pairs={{0,1},{1,2},{2,3},{3,4},{4,5},{5,6},{6,7},{7,8},{8,9},{9,10},{10,1... | collective-permute-start | bytes 6152 | tf_op jit(solution)/shard_map/ppermute | solution.py:459
  1.1 11.5 %collective-permute-start.2 = (s32[512]{0:T(512)}, s32[512]{0:T(512)S(1)}, u32[]{:S(2)}, u32[]{:S(2)}) collective-permute-start(s32[512]{0:T(512)} %param.9), channel_id=1, source_target_pairs={{0,0},{1,15},{2,14},{3,13},{4,12},{5,11},{6,10},{7,9},{8,8},{9,7},... | collective-permute-start | bytes 6152 | tf_op jit(solution)/shard_map/ppermute | solution.py:461
  2.5 10.8 %collective-permute-start.1 = (s32[512]{0:T(512)}, s32[512]{0:T(512)S(1)}, u32[]{:S(2)}, u32[]{:S(2)}) collective-permute-start(s32[512]{0:T(512)} %param.9), channel_id=1, source_target_pairs={{0,15},{1,14},{2,13},{3,12},{4,11},{5,10},{6,9},{7,8},{8,7},{9,6},... | collective-permute-start | bytes 6152 | tf_op jit(solution)/shard_map/ppermute | solution.py:460
  9.8 0.7 copy-start.8
  10.6 0.7 copy-start.3
  11.9 0.7 copy-start.7
  12.7 0.6 copy-start.5
  13.3 0.7 slice-start
  87.5 1.6 %copy-start = (f32[96,512]{1,0:T(8,128)S(1)}, f32[96,512]{1,0:T(8,128)}, u32[]{:S(2)}) copy-start(f32[96,512]{1,0:T(8,128)} %get-tuple-element.13) | copy-start | bytes 589828
  87.5 0.9 %copy-start.2 = (f32[2,3,512]{2,1,0:T(4,128)S(1)}, f32[2,3,512]{2,1,0:T(4,128)}, u32[]{:S(2)}) copy-start(f32[2,3,512]{2,1,0:T(4,128)} %get-tuple-element.21) | copy-start | bytes 36868
  89.1 0.8 copy-start.1
  91.2 0.7 copy-start.6
  91.9 0.7 copy-start.4

commit v4 on v3

--- a/solution.py
+++ b/solution.py
@@ -333,10 +333,10 @@
         hidden0_s[at, :] = (upward0 * gate0).astype(BF16)
         return carry
 
-    lax.fori_loop(0, 2 * half // 128, backward, 0)
-
+    lax.fori_loop(0, 1, backward, 0)
     first.finish(0)
     first.start(1)
+    lax.fori_loop(1, 2 * half // 128, backward, 0)
     rows_into(m_out0, low0_s, hidden0_s, lambda ref, cols=slice(None): ref[:, cols])
     second = Halving(n, order_b, me, (m_out0,), acc_b, send_b, recv_b, sems_b)
 
@@ -352,15 +352,13 @@
         ssend[j] = small_out[...]
         small_copy(j).start()
         second.start(j)
-        if j + 1 < steps:
-            if j > 0:
+        if j > 0:
+            first.finish(j)
+            if j + 1 < steps:
                 first.start(j + 1)
-            first.finish(j + 1) if j == 0 else None
         small_copy(j).wait()
         small_out[...] = small_out[...] + srecv[j]
         second.finish(j)
-        if 0 < j and j + 1 < steps:
-            first.finish(j + 1)
     out_a[...] = acc_a[0]
     out_b[...] = acc_b[0]
 

time: 93.6 us -> 81.1 us (0.87)
  Pallas kernels: 72.2 us -> 59.7 us
    pallas_call x1, Pallas kernels: 72.2 us -> 59.7 us  [fused(): pl.pallas_call(functools.partial(kernel, n, steps), out_shape=(jax.ShapeD...]
where the time goes in v4:
time: 81.1 us; the launch traced here: 80.7 us
  Pallas kernels  59.7 us (74%)
  starting transfers between devices  9.15 us (11%)
  local copies, waits for them, and re-layouts  8.68 us (11%)
  other arithmetic  2.21 us (3%)
  between operations  0.95 us (1%)
    pallas_call x1, Pallas kernels, fused(): pl.pallas_call(functools.partial(kernel, n, steps), out_shape=(jax.ShapeD...  59.7 us
    ppermute x1, starting transfers between devices, per_device(): tok_mirror = lax.ppermute(tokens, 'seq', to_mirror)  7.32 us
    unnamed x23, local copies, waits for them, and re-layouts  5.85 us
  transfers between devices with their start and end apart: 3, of which 0 were waited for; matrix products, arithmetic and copies ran while one was open for 1% of the time, Pallas kernels for 0%

profile of v4, /device:TPU:0, one launch (start us, length us, event | category | flops | bytes accessed | tf_op | source)
XLA Modules:
  0.0 80.7 jit_solution(11082251389048040895)
XLA Ops:
  0.6 0.5 collective-permute-start
  1.1 1.3 %collective-permute-start.2 = (s32[512]{0:T(512)}, s32[512]{0:T(512)S(1)}, u32[]{:S(2)}, u32[]{:S(2)}) collective-permute-start(s32[512]{0:T(512)} %param.9), channel_id=1, source_target_pairs={{0,0},{1,15},{2,14},{3,13},{4,12},{5,11},{6,10},{7,9},{8,8},{9,7},... | collective-permute-start | bytes 6152 | tf_op jit(solution)/shard_map/ppermute | solution.py:459
  2.5 7.3 %collective-permute-start.1 = (s32[512]{0:T(512)}, s32[512]{0:T(512)S(1)}, u32[]{:S(2)}, u32[]{:S(2)}) collective-permute-start(s32[512]{0:T(512)} %param.9), channel_id=1, source_target_pairs={{0,15},{1,14},{2,13},{3,12},{4,11},{5,10},{6,9},{7,8},{8,7},{9,6},... | collective-permute-start | bytes 6152 | tf_op jit(solution)/shard_map/ppermute | solution.py:458
  9.8 0.0 copy-start.8
  9.8 0.7 copy-done.8
  10.6 0.0 copy-start.3
  10.7 0.6 copy-done.3
  11.3 0.6 copy.15.taps
  11.9 0.0 copy-start.7
  11.9 0.0 collective-permute-done
  11.9 0.1 slice.37
  12.0 0.6 copy-done.7
  12.6 0.1 pad_add_fusion.1
  12.7 0.0 collective-permute-done.2
  12.7 0.0 copy-start.5
  12.7 0.6 copy-done.5
  13.3 0.0 collective-permute-done.1
  13.3 0.0 slice-start
  13.3 0.1 slice.39
  13.3 0.6 slice-done
  13.9 0.1 pad_add_fusion.2
  14.0 0.1 rev.7
  14.1 0.1 slice.47
  14.2 0.1 fusion
  14.3 0.1 rev.8
  14.5 0.1 constant_dynamic-slice_fusion.2
  14.6 0.7 reshape.51.codes
  15.3 59.7 %shard_map.136 = (f32[96,512]{1,0:T(8,128)}, f32[32,512]{1,0:T(8,128)}, f32[64,512]{1,0:T(8,128)}, f32[2,3,512]{2,1,0:T(4,128)}, f32[2,512]{1,0:T(2,128)}, /*index=5*/f32[4,512]{1,0:T(4,128)}) custom-call(s32[2]{0:T(128)} %dil.1, s32[16,1024]{1,0:T(8,128)} %reshape.51.codes, bf16[4,512]{1,0:T(4,128)(2,1)} %emb.1, f32[2,512]{1,0:T(2,128)} %gain.1, ...), custom_call_target="tpu_custom_call" | custom-call | tf_op jit(solution)/shard_map/pallas_call | solution.py:418
  75.0 0.0 copy-start
  75.1 0.0 copy-start.2
  75.1 0.9 %slice_bitcast_fusion.2 = (f32[1,32,512]{2,1,0:T(8,128)S(1)}, f32[1,32,512]{2,1,0:T(8,128)S(1)}) fusion(f32[64,512]{1,0:T(8,128)} %get-tuple-element.12), kind=kLoop, calls=%fused_computation.5 | loop fusion | bytes 262144 | tf_op jit(solution)/shard_map/unstack | solution.py:490
  76.0 0.0 copy-done.2
  76.0 0.6 copy.16
  76.6 0.0 copy-done
  76.6 0.0 copy-start.1
  76.6 0.8 %copy-done.1 = f32[32,512]{1,0:T(8,128)S(1)} copy-done((f32[32,512]{1,0:T(8,128)S(1)}, f32[32,512]{1,0:T(8,128)}, u32[]{:S(2)}) %copy-start.1) | copy-done | bytes 65560
  77.5 0.7 maximum_bitcast_fusion.2
  78.1 0.7 maximum_bitcast_fusion.1
  78.8 0.0 copy-start.6
  78.8 0.7 maximum_bitcast_fusion
  79.4 0.0 copy-done.6
  79.4 0.0 copy-start.4
  79.5 0.6 copy.20
  80.0 0.1 copy-done.4
  80.2 0.6 copy.21
  (12 shorter events, 0.1 us)
Async XLA Ops:
  0.6 11.3 %collective-permute-start = (s32[512]{0:T(512)}, s32[512]{0:T(512)S(1)}, u32[]{:S(2)}, u32[]{:S(2)}) collective-permute-start(s32[512]{0:T(512)} %param.9), channel_id=1, source_target_pairs={{0,1},{1,2},{2,3},{3,4},{4,5},{5,6},{6,7},{7,8},{8,9},{9,10},{10,1... | collective-permute-start | bytes 6152 | tf_op jit(solution)/shard_map/ppermute | solution.py:457
  1.1 11.5 %collective-permute-start.2 = (s32[512]{0:T(512)}, s32[512]{0:T(512)S(1)}, u32[]{:S(2)}, u32[]{:S(2)}) collective-permute-start(s32[512]{0:T(512)} %param.9), channel_id=1, source_target_pairs={{0,0},{1,15},{2,14},{3,13},{4,12},{5,11},{6,10},{7,9},{8,8},{9,7},... | collective-permute-start | bytes 6152 | tf_op jit(solution)/shard_map/ppermute | solution.py:459
  2.5 10.8 %collective-permute-start.1 = (s32[512]{0:T(512)}, s32[512]{0:T(512)S(1)}, u32[]{:S(2)}, u32[]{:S(2)}) collective-permute-start(s32[512]{0:T(512)} %param.9), channel_id=1, source_target_pairs={{0,15},{1,14},{2,13},{3,12},{4,11},{5,10},{6,9},{7,8},{8,7},{9,6},... | collective-permute-start | bytes 6152 | tf_op jit(solution)/shard_map/ppermute | solution.py:458
  9.8 0.7 copy-start.8
  10.6 0.7 copy-start.3
  11.9 0.7 copy-start.7
  12.7 0.6 copy-start.5
  13.3 0.7 slice-start
  75.0 1.6 %copy-start = (f32[96,512]{1,0:T(8,128)S(1)}, f32[96,512]{1,0:T(8,128)}, u32[]{:S(2)}) copy-start(f32[96,512]{1,0:T(8,128)} %get-tuple-element.13) | copy-start | bytes 589828
  75.1 0.9 %copy-start.2 = (f32[2,3,512]{2,1,0:T(4,128)S(1)}, f32[2,3,512]{2,1,0:T(4,128)}, u32[]{:S(2)}) copy-start(f32[2,3,512]{2,1,0:T(4,128)} %get-tuple-element.21) | copy-start | bytes 36868
  76.6 0.8 %copy-start.1 = (f32[32,512]{1,0:T(8,128)S(1)}, f32[32,512]{1,0:T(8,128)}, u32[]{:S(2)}) copy-start(f32[32,512]{1,0:T(8,128)} %get-tuple-element.14) | copy-start | bytes 196612
  78.8 0.7 copy-start.6
  79.4 0.7 copy-start.4
